TPU v7x, 32 devices: a whole 2x2x4 slice. The times are simulated.
32 devices in a mesh: seq: 8 (over z, y), exp: 4 (over x, core).
Axes of the slice: x: 2, y: 2, z: 4, core: 2. Of those that a mesh axis runs over, the one named last changes fastest.
Arguments:
- query_proj: bfloat16 [2048, 2048], P('seq', 'exp'), may hold values from -6 to 6
- key_proj: bfloat16 [2048, 2048], P('seq', 'exp'), may hold values from -6 to 6
- value_proj: bfloat16 [2048, 4096], P('seq', 'exp'), may hold values from -6 to 6
- result_valve_maps: bfloat16 [2048, 4096], P('seq', 'exp'), may hold values from -6 to 6
- beta_logit: float32 [2048, 32], P('seq', 'exp'), may hold values from -12 to 3
- decay_logit: float32 [2048, 32], P('seq', 'exp'), may hold values from -8 to 4126
- decay_rate: float32 [32], P('exp'), may hold values from 0 to 0.06
- conv_query: float32 [4, 2048], P(None, 'exp'), may hold values from -3 to 3
- conv_key: float32 [4, 2048], P(None, 'exp'), may hold values from -3 to 3
- conv_value: float32 [4, 4096], P(None, 'exp'), may hold values from -3 to 3
- norm_gain: float32 [128], replicated, may hold values from 0.1 to 1.9
- output_weight: bfloat16 [4096, 2048], P('exp'), may hold values from -0.09375 to 0.09375
- residual: bfloat16 [2048, 2048], P(('seq', 'exp')), may hold values from -6 to 6
- post_gain: float32 [2048], replicated, may hold values from 0.1 to 1.9
- route_experts: int32 [2048, 10], P(('seq', 'exp')), may hold values from 0 to 63, all different within a row; in each aligned block of 64 rows (0 to 63, 64 to 127, ...) at most 20 rows name the same one
- route_weights: float32 [2048, 10], P(('seq', 'exp')), may hold values from 0.05 to 1
- expert_gate: bfloat16 [64, 2048, 512], P(('seq', 'exp')), may hold values from -0.125 to 0.125
- expert_up: bfloat16 [64, 2048, 512], P(('seq', 'exp')), may hold values from -0.125 to 0.125
- expert_down: bfloat16 [64, 512, 2048], P(('seq', 'exp')), may hold values from -0.25 to 0.25
Outputs:
- mixer_out: bfloat16 [2048, 2048], P(('seq', 'exp'))
- expert_mixture: bfloat16 [2048, 2048], P(('seq', 'exp'))
Inputs may be any that keep to these rules, and one draw needn't show every extreme that they name: `route_experts`: each row names 10 different experts. Within the 64 rows of one device (aligned blocks of 64 rows) no expert is named more than 20 times, and in every draw some device names some expert exactly 20 times.
All inputs are finite; a program needn't handle non-finite values.
Results may differ from a plain program's by a relative error of at most 0.02.
Values may be sent and summed in bfloat16 or wider, within the bound.
A program may use at most 128 MiB of HBM per device.

v0:
```python
import jax
import jax.numpy as jnp
from jax import lax
from jax.sharding import PartitionSpec as P

BLOCK = 64


highest = lax.Precision.HIGHEST
epsilon = 1e-06


def carried_in(shard, axis, join, neutral):
    place = lax.axis_index(axis)
    gathered = jax.tree.map(
        lambda a, kind: lax.all_gather(a.astype(kind), axis), shard, (jnp.bfloat16, jnp.bfloat16)
    )
    state = jax.tree.map(lambda a, e: jnp.zeros_like(a) + jnp.asarray(e, a.dtype), shard, neutral)

    def one(lap, state):
        return join(
            state,
            jax.tree.map(
                lambda a, own: lax.dynamic_index_in_dim(a, lap, 0, False).astype(own.dtype),
                gathered,
                shard,
            ),
        )

    return lax.fori_loop(0, place, one, state)


def shifted(value, axis, steps):
    count = lax.axis_size(axis)
    leading, last = (max(0, -steps), min(count, count - steps))
    return lax.ppermute(value, axis, [(source, source + steps) for source in range(leading, last)])


def causal_conv(value_rows, kernel, leading):
    padded = jnp.concatenate([leading, value_rows], axis=0)
    length = value_rows.shape[0]
    running = jnp.zeros_like(value_rows)
    for offset in range(kernel.shape[0]):
        running = running + kernel[offset] * padded[offset : offset + length]
    return jax.nn.silu(running)


def block_terms(queries, key_rows, value_rows, beta_gate, log_decay):
    block_size = queries.shape[-2]
    cumulative = jnp.cumsum(log_decay, axis=-1)
    spread = cumulative[..., :, None] - cumulative[..., None, :]
    row_index = lax.broadcasted_iota(jnp.int32, (block_size, block_size), 0)
    col_index = lax.broadcasted_iota(jnp.int32, (block_size, block_size), 1)
    lower_mask = row_index >= col_index
    strict = row_index > col_index
    decay_mask = jnp.where(lower_mask, jnp.exp(jnp.where(lower_mask, spread, 0.0)), 0.0)
    key_key = jnp.einsum("...id,...jd->...ij", key_rows, key_rows, precision=highest)
    coupling = jnp.where(strict, beta_gate[..., :, None] * key_key * decay_mask, 0.0)
    identity = jnp.eye(block_size, dtype=jnp.float32)
    growth = jnp.exp(cumulative)
    stacked = jnp.concatenate(
        [beta_gate[..., None] * value_rows, (beta_gate * growth)[..., None] * key_rows], axis=-1
    )
    solved = jax.scipy.linalg.solve_triangular(
        identity + coupling, stacked, lower=True, unit_diagonal=True
    )
    payload_width = value_rows.shape[-1]
    updates = solved[..., :payload_width]
    key_mix = solved[..., payload_width:]
    scores = jnp.einsum("...id,...jd->...ij", queries, key_rows, precision=highest) * decay_mask
    local_out = jnp.einsum("...ij,...jv->...iv", scores, updates, precision=highest)
    lifted = growth[..., None] * queries - jnp.einsum(
        "...ij,...jd->...id", scores, key_mix, precision=highest
    )
    remain = jnp.exp(cumulative[..., -1:] - cumulative)
    key_tail = key_rows * remain[..., None]
    key_dim = key_rows.shape[-1]
    carry_map = jnp.exp(cumulative[..., -1])[..., None, None] * jnp.eye(
        key_dim, dtype=jnp.float32
    ) - jnp.einsum("...ci,...cj->...ij", key_mix, key_tail, precision=highest)
    write_term = jnp.einsum("...cv,...ck->...vk", updates, key_tail, precision=highest)
    return (local_out, lifted, carry_map, write_term)


def compose(earlier, later):
    early_map, early_memory = earlier
    late_map, late_memory = later
    joined_map = jnp.einsum("hij,hjk->hik", early_map, late_map, precision=highest)
    joined_memory = (
        jnp.einsum("hvj,hjk->hvk", early_memory, late_map, precision=highest) + late_memory
    )
    return (joined_map, joined_memory)


def incoming_memory(map_end, local_end, identity, empty):
    prior_map, prior_memory = carried_in((map_end, local_end), "seq", compose, (identity, empty))
    return prior_memory


def step_memory(memory, block_map, block_write):
    return jnp.einsum("hvd,hde->hve", memory, block_map, precision=highest) + block_write


def expert_mlp(arrived, expert_gate, expert_up, expert_down):
    gate_act = jnp.einsum(
        "secd,edf->secf", arrived, expert_gate, preferred_element_type=jnp.float32
    )
    up_act = jnp.einsum("secd,edf->secf", arrived, expert_up, preferred_element_type=jnp.float32)
    inner = (jax.nn.silu(gate_act) * up_act).astype(jnp.bfloat16)
    return jnp.einsum(
        "secf,efd->secd", inner, expert_down, preferred_element_type=jnp.float32
    ).astype(jnp.bfloat16)


def body(
    query_proj,
    key_proj,
    value_proj,
    result_valve_maps,
    beta_logit,
    decay_logit,
    decay_rate,
    conv_query,
    conv_key,
    conv_value,
    norm_gain,
    output_weight,
    residual,
    post_gain,
    route_experts,
    route_weights,
    expert_gate,
    expert_up,
    expert_down,
):
    tok_rows = query_proj.shape[0]
    head_dim = norm_gain.shape[0]
    rim_width = conv_query.shape[0] - 1
    key_cols = query_proj.shape[1]
    value_cols = value_proj.shape[1]
    edge = jnp.concatenate(
        [
            query_proj[tok_rows - rim_width :],
            key_proj[tok_rows - rim_width :],
            value_proj[tok_rows - rim_width :],
        ],
        axis=1,
    )
    leading = shifted(edge, "seq", 1).astype(jnp.float32)
    query_conv = causal_conv(query_proj.astype(jnp.float32), conv_query, leading[:, :key_cols])
    key_conv = causal_conv(
        key_proj.astype(jnp.float32), conv_key, leading[:, key_cols : 2 * key_cols]
    )
    value_conv = causal_conv(value_proj.astype(jnp.float32), conv_value, leading[:, 2 * key_cols :])
    key_heads = key_cols // head_dim
    value_heads = value_cols // head_dim
    key_split = key_conv.reshape(tok_rows, key_heads, head_dim)
    key_unit = key_split * lax.rsqrt(
        jnp.sum(key_split * key_split, axis=-1, keepdims=True) + epsilon
    )
    query_rep = jnp.repeat(query_conv.reshape(tok_rows, key_heads, head_dim), 2, axis=1)
    key_rep = jnp.repeat(key_unit, 2, axis=1)
    value_split = value_conv.reshape(tok_rows, value_heads, head_dim)
    beta_gate = jax.nn.sigmoid(beta_logit)
    log_decay = -decay_rate[None, :] * jax.nn.softplus(decay_logit)
    blocks = tok_rows // BLOCK

    def arrange(array):
        return array.reshape(blocks, BLOCK, value_heads, head_dim).transpose(0, 2, 1, 3)

    def arrange_gate(array):
        return array.reshape(blocks, BLOCK, value_heads).transpose(0, 2, 1)

    local_out, lifted, carry_map, write_term = block_terms(
        arrange(query_rep),
        arrange(key_rep),
        arrange(value_split),
        arrange_gate(beta_gate),
        arrange_gate(log_decay),
    )
    identity = jnp.broadcast_to(
        jnp.eye(head_dim, dtype=jnp.float32), (value_heads, head_dim, head_dim)
    )
    empty = jnp.zeros((value_heads, head_dim, head_dim), jnp.float32)

    def advance_maps(carry, block_item):
        memory, prefix = carry
        block_map, block_write = block_item
        memory = step_memory(memory, block_map, block_write)
        prefix = jnp.einsum("hij,hjk->hik", prefix, block_map, precision=highest)
        return ((memory, prefix), None)

    (local_end, map_end), _ = lax.scan(advance_maps, (empty, identity), (carry_map, write_term))
    prior_memory = incoming_memory(map_end, local_end, identity, empty)

    def advance_again(memory, block_item):
        block_out, block_lift, block_map, block_write = block_item
        result = block_out + jnp.einsum("hcd,hvd->hcv", block_lift, memory, precision=highest)
        memory = step_memory(memory, block_map, block_write)
        return (memory, result)

    _, core = lax.scan(advance_again, prior_memory, (local_out, lifted, carry_map, write_term))
    core = core.transpose(0, 2, 1, 3).reshape(tok_rows, value_heads, head_dim)
    gate_heads = result_valve_maps.astype(jnp.float32).reshape(tok_rows, value_heads, head_dim)
    mean_square = jnp.mean(core * core, axis=-1, keepdims=True)
    normed = (
        (core * lax.rsqrt(mean_square + epsilon) * norm_gain * jax.nn.silu(gate_heads))
        .astype(jnp.bfloat16)
        .reshape(tok_rows, value_cols)
    )
    rows_dev = residual.shape[0]
    model_dim = residual.shape[1]
    mixer = lax.psum_scatter(
        jnp.dot(normed, output_weight, preferred_element_type=jnp.float32).astype(jnp.bfloat16),
        "exp",
        scatter_dimension=0,
        tiled=True,
    ).astype(jnp.float32)
    mixer_out = (residual.astype(jnp.float32) + mixer).astype(jnp.bfloat16)
    mixed = mixer_out.astype(jnp.float32)
    moe_in = (
        mixed * lax.rsqrt(jnp.mean(mixed * mixed, axis=-1, keepdims=True) + epsilon) * post_gain
    ).astype(jnp.bfloat16)
    seq_count = lax.axis_size("seq")
    exp_count = lax.axis_size("exp")
    devices = seq_count * exp_count
    exp_dev = expert_gate.shape[0]
    expert_count = exp_dev * devices
    top_picks = route_experts.shape[1]
    capacity = 2 * ((rows_dev * top_picks + expert_count - 1) // expert_count)
    pick_count = rows_dev * top_picks
    linear_labels = route_experts.reshape(-1)
    expert_ids = jnp.arange(expert_count, dtype=jnp.int32)
    pick_table = (linear_labels[:, None] == expert_ids[None, :]).astype(jnp.bfloat16)
    row_index = lax.broadcasted_iota(jnp.int32, (pick_count, pick_count), 0)
    col_index = lax.broadcasted_iota(jnp.int32, (pick_count, pick_count), 1)
    earlier_picks = (row_index > col_index).astype(jnp.bfloat16)
    ranks = jnp.dot(earlier_picks, pick_table, preferred_element_type=jnp.float32)
    slot_index = jnp.take_along_axis(ranks, linear_labels[:, None], axis=1)[:, 0].astype(jnp.int32)
    position = linear_labels * capacity + slot_index
    source_row = (
        jnp.full((expert_count * capacity,), rows_dev, jnp.int32)
        .at[position]
        .set(jnp.arange(pick_count, dtype=jnp.int32) // top_picks)
    )
    padded_rows = jnp.concatenate([moe_in, jnp.zeros((1, model_dim), jnp.bfloat16)], axis=0)
    outgoing = padded_rows[source_row].reshape(devices, exp_dev, capacity, model_dim)
    finished = expert_mlp(
        lax.all_to_all(outgoing, ("seq", "exp"), split_axis=0, concat_axis=0, tiled=True),
        expert_gate,
        expert_up,
        expert_down,
    )
    returned = lax.all_to_all(finished, ("seq", "exp"), split_axis=0, concat_axis=0, tiled=True)
    flat_back = returned.reshape(expert_count * capacity, model_dim)
    picked = flat_back[position].reshape(rows_dev, top_picks, model_dim)
    shares = route_weights / jnp.sum(route_weights, axis=1, keepdims=True)
    expert_mixture = jnp.sum(picked.astype(jnp.float32) * shares[:, :, None], axis=1).astype(
        jnp.bfloat16
    )
    return (mixer_out, expert_mixture)


def solution(mesh):
    in_specs = (
        P("seq", "exp"),
        P("seq", "exp"),
        P("seq", "exp"),
        P("seq", "exp"),
        P("seq", "exp"),
        P("seq", "exp"),
        P("exp"),
        P(None, "exp"),
        P(None, "exp"),
        P(None, "exp"),
        P(),
        P("exp", None),
        P(("seq", "exp"), None),
        P(),
        P(("seq", "exp"), None),
        P(("seq", "exp"), None),
        P(("seq", "exp"), None, None),
        P(("seq", "exp"), None, None),
        P(("seq", "exp"), None, None),
    )
    out_specs = (P(("seq", "exp"), None), P(("seq", "exp"), None))
    return jax.shard_map(body, mesh=mesh, in_specs=in_specs, out_specs=out_specs, check_vma=False)
```

profile of v0, /device:TPU:0, one launch (start us, length us, event | category | flops | bytes accessed | tf_op | source)
XLA Modules:
  0.0 727.1 jit_solution(810139382420813456)
XLA Ops:
  9.4 4.9 collective-permute-start
  24.1 2.9 fusion.52
  27.0 158.1 %custom-call.4 = f32[4,8,1,64,64]{3,4,2,1,0:T(8,128)S(1)} custom-call(f32[4,8,1,64,64]{4,3,2,1,0:T(8,128)} %fusion.52), custom_call_target="InvertDiagBlocksLowerTriangular" | custom-call | tf_op jit(solution)/shard_map/jit(_solve_triangular)/vmap(vmap())/triangular_solve | solution.py:64
  185.8 2.0 fusion.38
  187.8 5.1 fusion.72
  193.0 5.4 multiply_subtract_fusion
  198.3 1.9 copy.134
  201.1 20.9 %while.39 = (s32[]{:T(128)}, f32[8,128,128]{1,2,0:T(8,128)}, f32[8,128,128]{1,2,0:T(8,128)}, f32[4,8,128,128]{2,3,1,0:T(8,128)S(1)}, f32[4,8,128,128]{2,3,1,0:T(8,128)}, /*index=5*/s32[]{:T(128)}, s32[]{:T(128)}) while((s32[]{:T(128)}, f32[8,128,128]{1,2,0:T(8,128)}, f32[8,128,128]{1,2,0:T(8,128)}, ...), condition=%wide.region_3.4_spmd.clone, body=%wide.region_2.3_spmd.clone.sunk | while | flops 402915328 | bytes 7865463 | solution.py:193
  202.2 2.5 fusion.164
  207.4 2.5 fusion.164
  212.5 2.5 fusion.164
  217.6 2.5 fusion.164
  222.0 1.9 copy.136
  224.0 1.9 copy.137
  226.9 2.0 copy_bitcast_fusion
  229.0 1.8 convolution_multiply_fusion
  230.8 2.2 fusion.73
  233.0 2.2 convolution_subtract_fusion
  235.2 38.5 %all-gather.5.cloned.1.call-done = bf16[64,128,128]{2,1,0:T(8,128)(2,1)} async-done(((bf16[8,128,128]{2,1,0:T(8,128)(2,1)}), bf16[64,128,128]{2,1,0:T(8,128)(2,1)}) %all-gather.5.cloned.1.call-update) | async-done | bytes 2097168 | tf_op jit(solution)/shard_map/all_gather | solution.py:16
  273.7 50.5 %all-gather.7.cloned.1.call-done = bf16[64,128,128]{2,1,0:T(8,128)(2,1)} async-done(((bf16[8,128,128]{2,1,0:T(8,128)(2,1)}), bf16[64,128,128]{2,1,0:T(8,128)(2,1)}) %all-gather.7.cloned.1.call-update) | async-done | bytes 2097168 | tf_op jit(solution)/shard_map/all_gather | solution.py:16
  324.3 16.6 %while.38 = (s32[]{:T(128)}, f32[8,128,128]{1,2,0:T(8,128)S(1)}, f32[4,8,64,128]{3,2,1,0:T(8,128)}, f32[4,8,128,128]{2,3,1,0:T(8,128)S(1)}, f32[4,8,128,128]{2,3...) while((s32[]{:T(128)}, f32[8,128,128]{1,2,0:T(8,128)S(1)}, ...), condition=%wide.region_7.8_spmd, body=%wide.region_6.7_spmd.sunk | while | flops 302186496 | bytes 4458581 | solution.py:202
  324.3 2.4 fusion.159
  326.7 1.7 fusion.158
  328.5 2.4 fusion.159
  330.8 1.7 fusion.158
  332.6 2.4 fusion.159
  336.8 2.4 fusion.159
  339.2 1.7 fusion.158
  342.6 1.8 copy.144
  344.8 4.7 convolution_convert_fusion
  350.6 5.4 gather_fusion.2
  356.1 4.1 scatter_custom_fusion
  360.3 31.4 %reduce-scatter.2.cloned.1.call-done = bf16[64,2048]{1,0:T(8,128)(2,1)} async-done(((bf16[256,2048]{1,0:T(8,128)(2,1)}), bf16[64,2048]{1,0:T(8,128)(2,1)}) %reduce-scatter.2.cloned.1.call-update) | async-done | bytes 262160 | tf_op jit(solution)/shard_map/reduce_scatter | solution.py:213
  393.0 6.2 gather_fusion
  399.2 8.9 %reshape.274 = bf16[32,2,20,2048]{3,2,1,0:T(8,128)(2,1)} reshape(bf16[1280,2048]{1,0:T(8,128)(2,1)} %gather_fusion) | data formatting | bytes 10485760 | tf_op jit(solution)/shard_map/reshape | solution.py:247
  408.1 9.7 %copy.150 = bf16[32,2,20,2048]{3,1,2,0:T(2,128)(2,1)S(1)} copy(bf16[32,2,20,2048]{3,2,1,0:T(8,128)(2,1)} %reshape.274) | data formatting | bytes 10485760 | tf_op jit(solution)/shard_map/reshape | solution.py:247
  417.9 120.7 %all_to_all.10 = bf16[32,2,20,2048]{3,1,2,0:T(2,128)(2,1)S(1)} all-to-all(bf16[32,2,20,2048]{3,1,2,0:T(2,128)(2,1)S(1)} %copy.150), channel_id=1, replica_groups=mesh['seq'=8,'exp'=4] {'seq','exp'}, dimensions={0} | all-to-all | bytes 10485760 | tf_op jit(solution)/shard_map/all_to_all | solution.py:249
  538.6 4.5 fusion.24
  543.1 4.8 fusion.34
  547.9 4.8 convert_bitcast_fusion
  552.7 10.2 %copy.154 = bf16[32,2,20,2048]{3,1,2,0:T(2,128)(2,1)} copy(bf16[32,2,20,2048]{3,0,2,1:T(8,128)(2,1)} %convert_bitcast_fusion) | data formatting | bytes 10485760 | tf_op jit(solution)/shard_map/convert_element_type | solution.py:112
  562.9 4.1 all-to-all-start.1
  567.2 116.6 %all-to-all-done.1 = bf16[32,2,20,2048]{3,1,2,0:T(2,128)(2,1)} async-done(((bf16[32,2,20,2048]{3,1,2,0:T(2,128)(2,1)}), bf16[32,2,20,2048]{3,1,2,0:T(2,128)(2,1)}, u32[]{:S(2)}, u32[]{:S(2)}) %all-to-all-start.1) | async-done | bytes 5242912 | tf_op jit(solution)/shard_map/all_to_all | solution.py:254
  683.8 7.8 %copy.155 = bf16[32,2,20,2048]{3,2,1,0:T(8,128)(2,1)} copy(bf16[32,2,20,2048]{3,1,2,0:T(2,128)(2,1)} %all-to-all-done.1) | data formatting | bytes 10485760 | tf_op jit(solution)/shard_map/all_to_all | solution.py:254
  691.6 9.0 %reshape.275 = bf16[1280,2048]{1,0:T(8,128)(2,1)} reshape(bf16[32,2,20,2048]{3,2,1,0:T(8,128)(2,1)} %copy.155) | data formatting | bytes 10485760 | tf_op jit(solution)/shard_map/reshape | solution.py:255
  700.6 9.5 %gather_fusion.1 = bf16[640,2048]{1,0:T(8,128)(2,1)S(1)} fusion(bf16[1280,2048]{1,0:T(8,128)(2,1)} %reshape.275, s32[1024]{0:T(1024)S(1)} %pad_clamp_fusion.1), kind=kCustom, calls=%fused_computation.1 | custom fusion | bytes 5245440 | tf_op jit(solution)/shard_map/gather | solution.py:256
  710.1 3.7 reshape.277
  713.8 6.6 multiply_reduce_fusion
  (133 shorter events, 31.5 us)
Async XLA Ops:
  7.2 219.7 %copy-start = (f32[128]{0:T(128)S(1)}, f32[128]{0:T(128)}, u32[]{:S(2)}) copy-start(f32[128]{0:T(128)} %param.35) | copy-start | bytes 1540
  7.2 266.5 %all-gather.5.cloned.1.call-start = ((), (), s32[]{:S(2)}) async-start(), calls=%async_computation.4 | async-start | bytes 2359296 | tf_op jit(solution)/shard_map/all_gather | solution.py:16
  9.4 12.5 %collective-permute-start = (bf16[3,2048]{1,0:T(4,128)(2,1)S(1)}, bf16[3,2048]{1,0:T(4,128)(2,1)S(1)}, u32[]{:S(2)}, u32[]{:S(2)}) collective-permute-start(bf16[3,2048]{1,0:T(4,128)(2,1)S(1)} %pad_maximum_fusion.3), channel_id=1, source_target_pairs={{0,4},{4,8},{8,12},{12,16},{16,20},{20,24},{24,28},{1,5},{5,9},{9,... | collective-permute-start | bytes 36872 | tf_op jit(solution)/shard_map/ppermute | solution.py:36
  187.8 5.1 copy-start.3
  201.1 24.9 %copy-start.6 = (bf16[256,512]{1,0:T(8,128)(2,1)S(1)}, bf16[256,512]{1,0:T(8,128)(2,1)}, u32[]{:S(2)}) copy-start(bf16[256,512]{1,0:T(8,128)(2,1)} %param.25) | copy-start | bytes 786436
  201.1 25.7 %copy-start.11 = (f32[4,512]{1,0:T(4,128)S(1)}, f32[4,512]{1,0:T(4,128)}, u32[]{:S(2)}) copy-start(f32[4,512]{1,0:T(4,128)} %param.32) | copy-start | bytes 24580
  201.1 3.6 copy-start.2
  206.3 3.6 copy-start.2
  211.4 3.6 copy-start.2
  216.5 3.6 copy-start.2
  224.0 100.3 %all-gather.7.cloned.1.call-start = ((), (), s32[]{:S(2)}) async-start(), calls=%async_computation.5 | async-start | bytes 2359296 | tf_op jit(solution)/shard_map/all_gather | solution.py:16
  225.9 165.7 %reduce-scatter.2.cloned.1.call-start = ((), (), s32[]{:S(2)}) async-start(), calls=%async_computation.3 | async-start | bytes 1310720 | tf_op jit(solution)/shard_map/reduce_scatter | solution.py:213
  226.8 4.0 copy-start.4
  340.9 3.9 copy-start.15
  344.8 4.7 copy-start.10
  349.5 42.1 %copy-start.7 = (bf16[64,2048]{1,0:T(8,128)(2,1)S(1)}, bf16[64,2048]{1,0:T(8,128)(2,1)}, u32[]{:S(2)}) copy-start(bf16[64,2048]{1,0:T(8,128)(2,1)} %param.37) | copy-start | bytes 786436
  349.6 43.3 %copy-start.9 = (f32[2048]{0:T(1024)S(1)}, f32[2048]{0:T(1024)}, u32[]{:S(2)}) copy-start(f32[2048]{0:T(1024)} %param.38) | copy-start | bytes 24580
  392.8 6.4 copy-start.5
  417.9 120.7 %copy-start.12 = (bf16[2,2048,512]{2,1,0:T(8,128)(2,1)S(1)}, bf16[2,2048,512]{2,1,0:T(8,128)(2,1)}, u32[]{:S(2)}) copy-start(bf16[2,2048,512]{2,1,0:T(8,128)(2,1)} %param.42) | copy-start | bytes 12582916
  538.6 4.5 copy-start.13
  543.1 4.8 copy-start.14
  562.9 4.1 copy-start.8
  562.9 120.9 %all-to-all-start.1 = ((bf16[32,2,20,2048]{3,1,2,0:T(2,128)(2,1)}), bf16[32,2,20,2048]{3,1,2,0:T(2,128)(2,1)}, u32[]{:S(2)}, u32[]{:S(2)}) async-start(bf16[32,2,20,2048]{3,1,2,0:T(2,128)(2,1)} %copy.154), calls=%async_computation.2 | async-start | bytes 10485760 | tf_op jit(solution)/shard_map/all_to_all | solution.py:254
  710.1 10.3 %copy-start.1 = (f32[128]{0:T(128)S(1)}, f32[128]{0:T(128)}, u32[]{:S(2)}) copy-start(f32[128]{0:T(128)} %param.35) | copy-start | bytes 1540
Sparse Core Ops, SparseCore 0:
  224.1 49.5 all-gather.4
  276.4 47.7 all-gather.6
  349.7 41.9 reduce-scatter.1
where the time goes:
time: 733 us; the launch traced here: 727 us
  waiting for transfers between devices  237 us (32%)
  other arithmetic  178 us (24%)
  blocking collectives  121 us (17%)
  local copies, waits for them, and re-layouts  93.6 us (13%)
  matrix products  73.2 us (10%)
  between operations  14.6 us (2%)
  starting transfers between devices  9.13 us (1%)
    another operation x4, other arithmetic, block_terms(): jax.scipy.linalg.solve_triangular(identity + coupling, stacked, lower=Tru...  158 us
    all_to_all x1, blocking collectives, body(): lax.all_to_all(outgoing, ('seq', 'exp'), split_axis=0, concat_axis=0, til...  121 us
    all_to_all x1, waiting for transfers between devices, body(): lax.all_to_all(finished, ('seq', 'exp'), split_axis=0, concat_axis=0, til...  117 us
    all_gather x2, waiting for transfers between devices, carried_in(): lax.all_gather(a.astype(kind), axis)  89 us
    reduce_scatter x1, waiting for transfers between devices, body(): lax.psum_scatter(jnp.dot(normed, output_weight, preferred_element_type=jn...  31.4 us
    reshape x2, local copies, waits for them, and re-layouts, body(): padded_rows[source_row].reshape(devices, exp_dev, capacity, model_dim)  18.7 us
    dot_general x8, matrix products, step_memory(): jnp.einsum('hvd,hde->hve', memory, block_map, precision=highest)  16.9 us
  transfers between devices with their start and end apart: 5, of which 4 were waited for; matrix products, arithmetic and copies ran while one was open for 4% of the time, Pallas kernels for 0%

commit v1 on v0

v1 whole, which is shorter than its diff:
```python
import functools

import jax
import jax.numpy as jnp
from jax import lax
from jax.experimental import pallas as pl
from jax.experimental.pallas import tpu as pltpu
from jax.sharding import PartitionSpec as P

epsilon = 1e-06
f32 = jnp.float32
bf16 = jnp.bfloat16
MESH = pl.DeviceIdType.MESH
NN = (((1,), (0,)), ((), ()))
NT = (((1,), (1,)), ((), ()))
TN = (((0,), (0,)), ((), ()))
VMEM = pl.BlockSpec(memory_space=pltpu.VMEM)
ANY = pl.BlockSpec(memory_space=pl.ANY)


def shifted(value, axis, steps):
    count = lax.axis_size(axis)
    leading, last = (max(0, -steps), min(count, count - steps))
    return lax.ppermute(value, axis, [(source, source + steps) for source in range(leading, last)])


def silu(x):
    return x / (1.0 + jnp.exp(-x))


def mm(a, b, dims=NN):
    return lax.dot_general(a, b, dims, preferred_element_type=f32)


def split(x):
    high = x.astype(bf16)
    return high, (x - high.astype(f32)).astype(bf16)


def dot3(a, b, dims=NN):
    ah, al = split(a)
    bh, bl = split(b)
    return mm(ah, bh, dims) + (mm(ah, bl, dims) + mm(al, bh, dims))


def conv_act(x_ref, halo_ref, w_ref):
    taps = w_ref.shape[0]
    rows = x_ref.shape[0]
    top = halo_ref.shape[0]
    padded = jnp.concatenate([halo_ref[...], x_ref[...].astype(f32)], axis=0)
    total = w_ref[taps - 1 : taps, :] * padded[top : top + rows]
    for j in range(taps - 1):
        start = top - (taps - 1) + j
        total = total + w_ref[j : j + 1, :] * padded[start : start + rows]
    return silu(total)


def local_kernel(
    hd, q_ref, k_ref, v_ref, hq_ref, hk_ref, hv_ref, wq_ref, wk_ref, wv_ref,
    beta_ref, cum_ref, cumt_ref, lo_ref, lift_ref, map_ref, write_ref, coup, inv, score,
):
    rows = q_ref.shape[0]
    key_heads = q_ref.shape[1] // hd
    heads = v_ref.shape[1] // hd
    per = heads // key_heads
    q = conv_act(q_ref, hq_ref, wq_ref)
    k = conv_act(k_ref, hk_ref, wk_ref)
    v = conv_act(v_ref, hv_ref, wv_ref)
    ri = lax.broadcasted_iota(jnp.int32, (rows, rows), 0)
    ci = lax.broadcasted_iota(jnp.int32, (rows, rows), 1)
    apart = ri ^ ci
    low = ri >= ci
    strict = ri > ci
    qs, ks = [], []
    for a in range(key_heads):
        ka = k[:, a * hd : (a + 1) * hd]
        ka = ka * lax.rsqrt(jnp.sum(ka * ka, axis=1, keepdims=True) + epsilon)
        qa = q[:, a * hd : (a + 1) * hd]
        qs.append(qa)
        ks.append(ka)
        kk = dot3(ka, ka, NT)
        qk = dot3(qa, ka, NT)
        for h in range(a * per, (a + 1) * per):
            spread = (cum_ref[:, h : h + 1] - cumt_ref[h : h + 1, :]) + (
                cum_ref[:, heads + h : heads + h + 1] - cumt_ref[heads + h : heads + h + 1, :]
            )
            decay = jnp.where(low, jnp.exp(jnp.where(low, spread, 0.0)), 0.0)
            coupling = jnp.where(strict, beta_ref[:, h : h + 1] * kk * decay, 0.0)
            coup[h] = coupling
            score[h] = qk * decay
            inv[h] = jnp.where(ri == ci, 1.0, 0.0) - jnp.where(apart == 1, coupling, 0.0)

    half = rows // 2
    near_bits = apart[:half, :half]

    def level(step, carry):
        near = lax.shift_right_logical(near_bits, jnp.full_like(near_bits, step)) == 1
        for h in range(heads):
            for part in (slice(0, half), slice(half, rows)):
                x = inv[h, part, part]
                c = jnp.where(near, coup[h, part, part], 0.0)
                inv[h, part, part] = x - dot3(x, dot3(c, x))
        return carry

    lax.fori_loop(1, (half - 1).bit_length(), level, 0)
    for h in range(heads):
        inv[h, half:, :half] = -dot3(inv[h, half:, half:], dot3(coup[h, half:, :half], inv[h, :half, :half]))
    eye = jnp.where(
        lax.broadcasted_iota(jnp.int32, (hd, hd), 0) == lax.broadcasted_iota(jnp.int32, (hd, hd), 1), 1.0, 0.0
    )
    for h in range(heads):
        cum = cum_ref[:, h : h + 1] + cum_ref[:, heads + h : heads + h + 1]
        growth = jnp.exp(cum)
        last_w = cum_ref[rows - 1 : rows, h : h + 1]
        last_f = cum_ref[rows - 1 : rows, heads + h : heads + h + 1]
        remain = jnp.exp(
            (last_w - cum_ref[:, h : h + 1]) + (last_f - cum_ref[:, heads + h : heads + h + 1])
        )
        beta = beta_ref[:, h : h + 1]
        qa, ka = qs[h // per], ks[h // per]
        stacked = jnp.concatenate([beta * v[:, h * hd : (h + 1) * hd], (beta * growth) * ka], axis=1)
        solved = dot3(inv[h], stacked)
        mixed = dot3(score[h], solved)
        lo_ref[:, h * hd : (h + 1) * hd] = mixed[:, :hd]
        lift_ref[:, h * hd : (h + 1) * hd] = growth * qa - mixed[:, hd:]
        ends = dot3(solved, ka * remain, TN)
        write_ref[h] = ends[:hd]
        map_ref[h] = jnp.exp(last_w + last_f) * eye - ends[hd:]


def local_terms(q, k, v, halo, wq, wk, wv, beta, log_decay, hd):
    rows, kc = q.shape
    vc = v.shape[1]
    heads = vc // hd
    groups = 2 if (kc // hd) % 2 == 0 else 1
    gh = heads // groups
    kw, vw = kc // groups, vc // groups
    bounded = jnp.maximum(log_decay, -110.0)
    whole = jnp.floor(bounded)
    sums = jnp.cumsum(jnp.stack([whole, bounded - whole]), axis=1)
    cum = sums.reshape(2, rows, groups, gh).transpose(2, 1, 0, 3).reshape(groups, rows, 2 * gh)
    cumt = sums.reshape(2, rows, groups, gh).transpose(2, 0, 3, 1).reshape(groups, 2 * gh, rows)
    betag = beta.reshape(rows, groups, gh).transpose(1, 0, 2)
    taps = wq.shape[0]
    halo = jnp.concatenate([jnp.zeros((8 - halo.shape[0], halo.shape[1]), f32), halo], axis=0)
    hq, hk, hv = halo[:, :kc], halo[:, kc : 2 * kc], halo[:, 2 * kc :]
    col = lambda r, w: pl.BlockSpec((r, w), lambda g: (0, g))
    lead = lambda a, b: pl.BlockSpec((None, a, b), lambda g: (g, 0, 0))
    mats = pl.BlockSpec((gh, hd, hd), lambda g: (g, 0, 0))
    return pl.pallas_call(
        functools.partial(local_kernel, hd),
        grid=(groups,),
        in_specs=[
            col(rows, kw), col(rows, kw), col(rows, vw), col(8, kw), col(8, kw), col(8, vw),
            col(taps, kw), col(taps, kw), col(taps, vw),
            lead(rows, gh), lead(rows, 2 * gh), lead(2 * gh, rows),
        ],
        out_specs=[col(rows, vw), col(rows, vw), mats, mats],
        out_shape=[
            jax.ShapeDtypeStruct((rows, vc), f32),
            jax.ShapeDtypeStruct((rows, vc), f32),
            jax.ShapeDtypeStruct((heads, hd, hd), f32),
            jax.ShapeDtypeStruct((heads, hd, hd), f32),
        ],
        scratch_shapes=[pltpu.VMEM((gh, rows, rows), f32)] * 3,
        compiler_params=pltpu.CompilerParams(vmem_limit_bytes=60 << 20),
        name="block_terms",
    )(q, k, v, hq, hk, hv, wq, wk, wv, betag, cum, cumt)


def mixer_kernel(
    ns, ne, gather, lo_ref, lift_ref, map_ref, write_ref, valve_ref, gain_ref, w_ref, res_ref, post_ref, share_ref,
    out_ref, tok_ref, state_in, state_out, normed, partial, wire, near_in, cross_out, cross_in, payload,
    st_send, st_recv, rs_send, rs_recv, xs_send, xs_recv, ag_send, ag_recv, own_sem,
):
    s = lax.axis_index("seq")
    e = lax.axis_index("exp")
    heads, hd, _ = map_ref.shape
    rows = res_ref.shape[0]
    dim = res_ref.shape[1]
    na = ne // 2
    a, c = e // 2, e % 2
    barrier = pltpu.get_barrier_semaphore()
    for i in range(1, ns):
        pl.semaphore_signal(barrier, inc=1, device_id=((s + i) % ns, e), device_id_type=MESH)
    for i in range(1, ne):
        pl.semaphore_signal(barrier, inc=1, device_id=(s, (e + i) % ne), device_id_type=MESH)
    pl.semaphore_wait(barrier, ns + ne - 2)

    def chain(h):
        return pltpu.make_async_remote_copy(
            src_ref=state_out.at[h], dst_ref=state_in.at[h], send_sem=st_send.at[h], recv_sem=st_recv.at[h],
            device_id=((s + 1) % ns, e), device_id_type=MESH,
        )

    @pl.when(s == 0)
    def _():
        state_in[...] = jnp.zeros_like(state_in)

    for h in range(heads):
        mh, ml = split(map_ref[h])

        @pl.when(s > 0)
        def _():
            chain(h).wait_recv()

        memory = state_in[h]
        state_out[h] = (mm(memory, mh) + mm(memory, ml) + write_ref[h]).astype(bf16)

        @pl.when(s < ns - 1)
        def _():
            chain(h).start()

    for h in range(heads):
        cols = slice(h * hd, (h + 1) * hd)
        memory = state_in[h]
        lh, ll = split(lift_ref[:, cols])
        core = lo_ref[:, cols] + (mm(lh, memory, NT) + mm(ll, memory, NT))
        mean = jnp.mean(core * core, axis=1, keepdims=True)
        valve = valve_ref[:, cols].astype(f32)
        normed[:, cols] = (core * lax.rsqrt(mean + epsilon) * gain_ref[...] * silu(valve)).astype(bf16)

    chunk = dim // 4
    for n in range(4):
        cols = slice(n * chunk, (n + 1) * chunk)
        product = mm(normed[...], w_ref[:, cols])
        for b in range(ne):
            partial[b, :, cols] = product[b * rows : (b + 1) * rows]
            wire[b, :, cols] = product[b * rows : (b + 1) * rows].astype(bf16)

    def near(i):
        there = (a + i) % na
        return pltpu.make_async_remote_copy(
            src_ref=wire.at[there * 2 + 1 - c], dst_ref=near_in.at[there], send_sem=rs_send.at[i], recv_sem=rs_recv.at[i],
            device_id=(s, a * 2 + 1 - c), device_id_type=MESH,
        )

    def cross(i):
        there = (a + i) % na
        return pltpu.make_async_remote_copy(
            src_ref=cross_out.at[i - 1], dst_ref=cross_in.at[i - 1], send_sem=xs_send.at[i - 1], recv_sem=xs_recv.at[i - 1],
            device_id=(s, there * 2 + c), device_id_type=MESH,
        )

    for i in range(na):
        near((i + 1) % na).start()
    for i in range(1, na):
        there = (a + i) % na
        near(i).wait_recv()
        cross_out[i - 1] = (partial[there * 2 + c] + near_in[there].astype(f32)).astype(bf16)
        cross(i).start()
    near(0).wait_recv()
    total = partial[e] + near_in[a].astype(f32)
    for i in range(1, na):
        cross(i).wait_recv()
        total = total + cross_in[i - 1].astype(f32)
    result = (res_ref[...].astype(f32) + total).astype(bf16)
    out_ref[...] = result
    mixed = result.astype(f32)
    tokens = (
        mixed * lax.rsqrt(jnp.mean(mixed * mixed, axis=1, keepdims=True) + epsilon) * post_ref[...]
    ).astype(bf16)
    sends = []
    if gather:
        payload[:, :dim] = tokens
        payload[:, dim:] = share_ref[...]
        nz = ns // 2
        z, y = s // 2, s % 2
        here = (z, y, a, c)
        half = dim // 2
        spans = (pl.ds(0, half), pl.ds(half, payload.shape[1] - half))

        def slot(p):
            return ((p[0] * 2 + p[1]) * na + p[2]) * 2 + p[3]

        own = pltpu.make_async_copy(payload, tok_ref.at[slot(here)], own_sem)
        own.start()

        def send(part, place, target, mine):
            index = slot(place)
            number = sum(1 for other, _ in sends if other == part)
            source = payload if mine else tok_ref.at[index]
            copy = pltpu.make_async_remote_copy(
                src_ref=source.at[:, spans[part]], dst_ref=tok_ref.at[index, :, spans[part]],
                send_sem=ag_send.at[part, number], recv_sem=ag_recv.at[part, index],
                device_id=(target[0] * 2 + target[1], target[2] * 2 + target[3]), device_id_type=MESH,
            )
            copy.start()
            sends.append((part, copy))

        def arrive(part, place):
            index = slot(place)
            pltpu.make_async_remote_copy(
                src_ref=payload.at[:, spans[part]], dst_ref=tok_ref.at[index, :, spans[part]],
                send_sem=ag_send.at[part, 0], recv_sem=ag_recv.at[part, index],
                device_id=(s, a * 2 + 1 - c), device_id_type=MESH,
            ).wait_recv()

        ypeer = (z, 1 - y, a, c)
        xpeer = (z, y, 1 - a, c)
        cpeer = (z, y, a, 1 - c)
        first, second = (ypeer, xpeer), (xpeer, ypeer)
        zs = [(z + i) % nz for i in range(nz)]
        back = [(z - i + nz) % nz for i in range(nz)]
        for i in range(1, nz):
            for part in (0, 1):
                send(part, here, (zs[i], y, a, c), True)
        for peers in (first, second, (cpeer, cpeer)):
            for part in (0, 1):
                send(part, here, peers[part], True)
        for i in range(1, nz):
            for part in (0, 1):
                place = (back[i], y, a, c)
                arrive(part, place)
                send(part, place, first[part], False)
                send(part, place, second[part], False)
                send(part, place, cpeer, False)
        for i in range(nz):
            for part in (0, 1):
                place = (back[i],) + first[part][1:]
                arrive(part, place)
                send(part, place, second[part], False)
                send(part, place, cpeer, False)
        for via in (0, 1):
            for i in range(nz):
                for part in (0, 1):
                    place = (back[i],) + second[part][1:]
                    if via:
                        place = (back[i], 1 - y, 1 - a, c)
                    arrive(part, place)
                    send(part, place, cpeer, False)
        for yy in (y, 1 - y):
            for aa in (a, 1 - a):
                for i in range(nz):
                    for part in (0, 1):
                        arrive(part, (back[i], yy, aa, 1 - c))
        own.wait()
    else:
        tok_ref[...] = tokens
    for _, copy in sends:
        copy.wait_send()
    for h in range(heads):
        @pl.when(s < ns - 1)
        def _():
            chain(h).wait_send()
    for i in range(na):
        near(i).wait_send()
    for i in range(1, na):
        cross(i).wait_send()


def mixer_call(ns, ne, gather, lo, lift, maps, writes, valve, gain, weight, residual, post, shares):
    heads, hd, _ = maps.shape
    tok_rows = lo.shape[0]
    rows, dim = residual.shape
    na = ne // 2
    width = dim + shares.shape[1]
    dma = pltpu.SemaphoreType.DMA
    tok_shape = (ns * ne, rows, width) if gather else (rows, dim)
    sent = (ns // 2 - 1) + 3 + 3 * (ns // 2 - 1) + 2 * (ns // 2) + 2 * (ns // 2)
    return pl.pallas_call(
        functools.partial(mixer_kernel, ns, ne, gather),
        in_specs=[VMEM] * 10,
        out_specs=[VMEM, ANY if gather else VMEM],
        out_shape=[jax.ShapeDtypeStruct((rows, dim), bf16), jax.ShapeDtypeStruct(tok_shape, bf16)],
        scratch_shapes=[
            pltpu.VMEM((heads, hd, hd), bf16), pltpu.VMEM((heads, hd, hd), bf16),
            pltpu.VMEM((tok_rows, heads * hd), bf16),
            pltpu.VMEM((ne, rows, dim), f32), pltpu.VMEM((ne, rows, dim), bf16),
            pltpu.VMEM((na, rows, dim), bf16),
            pltpu.VMEM((na - 1, rows, dim), bf16), pltpu.VMEM((na - 1, rows, dim), bf16),
            pltpu.VMEM((rows, width), bf16),
            dma((heads,)), dma((heads,)), dma((na,)), dma((na,)), dma((na - 1,)), dma((na - 1,)),
            dma((2, sent)), dma((2, ns * ne)), dma,
        ],
        compiler_params=pltpu.CompilerParams(
            collective_id=0, has_side_effects=True, vmem_limit_bytes=60 << 20
        ),
        name="mixer_tail",
    )(lo, lift, maps, writes, valve, gain, weight, residual, post, shares)


def expert_kernel(
    ns, ne, tok_ref, gate_hbm, up_hbm, down_hbm, sel_ref, out_ref, gate, up, down, xbuf, part, near_in, acc1,
    in_a, in_b, acc2a, acc2b, in2_a, in2_b, acc3, in3, w_sem, x_sem,
    n_send, n_recv, a_send, a_recv, b_send, b_recv, a2_send, a2_recv, b2_send, b2_recv, z_send, z_recv,
):
    s = lax.axis_index("seq")
    e = lax.axis_index("exp")
    nz = ns // 2
    z, y = s // 2, s % 2
    a, c = e // 2, e % 2
    own = gate.shape[0]
    rows, dim = out_ref.shape
    half = dim // 2
    lo, hi = pl.ds(0, half), pl.ds(half, half)
    yo, ao = 1 - y, 1 - a
    ypeer = (z * 2 + yo, e)
    xpeer = (s, ao * 2 + c)
    cpeer = (s, a * 2 + 1 - c)

    def load(i, kind):
        held, source = ((gate, gate_hbm), (up, up_hbm), (down, down_hbm))[kind]
        return pltpu.make_async_copy(source.at[i], held.at[i], w_sem.at[kind, i])

    def fetch(k, yy, place):
        return pltpu.make_async_copy(tok_ref.at[pl.ds((k * 2 + yy) * ne, ne)], xbuf.at[place], x_sem.at[place])

    def at(j):
        return (z + 1 + j) % nz

    fetch(at(0), yo, 0).start()
    for i in range(own):
        for kind in range(3):
            load(i, kind).start()
    barrier = pltpu.get_barrier_semaphore()
    peers = [ypeer, xpeer, cpeer] + [(((z + i) % nz) * 2 + y, e) for i in range(1, nz)]
    for peer in peers:
        pl.semaphore_signal(barrier, inc=1, device_id=peer, device_id_type=MESH)
    pl.semaphore_wait(barrier, len(peers))

    def copy(src, dst, ss, rs, to):
        return pltpu.make_async_remote_copy(
            src_ref=src, dst_ref=dst, send_sem=ss, recv_sem=rs, device_id=to, device_id_type=MESH
        )

    def near(k, yy, aa):
        f = (k * 2 + yy) * 2 + aa
        return copy(part.at[f * 2 + 1 - c], near_in.at[f], n_send.at[f], n_recv.at[f], cpeer)

    def step_a(k, yy):
        i = k * 2 + yy
        return copy(acc1.at[i * 2 + ao, :, lo], in_a.at[i], a_send.at[i], a_recv.at[i], xpeer)

    def step_b(k, aa):
        i = k * 2 + aa
        return copy(acc1.at[(k * 2 + yo) * 2 + aa, :, hi], in_b.at[i], b_send.at[i], b_recv.at[i], ypeer)

    def step_a2(k):
        return copy(acc2a.at[k * 2 + yo], in2_a.at[k], a2_send.at[k], a2_recv.at[k], ypeer)

    def step_b2(k):
        return copy(acc2b.at[k * 2 + ao], in2_b.at[k], b2_send.at[k], b2_recv.at[k], xpeer)

    def last(j):
        k = at(j)
        return copy(acc3.at[j], in3.at[j], z_send.at[j], z_recv.at[j], (k * 2 + y, e))

    def tile(k, yy, place, first):
        x = xbuf[place].reshape(ne * rows, xbuf.shape[-1])
        spread = x[:, dim:].astype(f32)
        inners = []
        for i in range(own):
            if first is not None:
                @pl.when(first)
                def _():
                    load(i, 0).wait()
                    load(i, 1).wait()
            share = jnp.sum(spread * sel_ref[i : i + 1, :], axis=1, keepdims=True)
            g = mm(x[:, :dim], gate[i])
            u = mm(x[:, :dim], up[i])
            inners.append((silu(g) * u * share).astype(bf16))
        if first is not None:
            @pl.when(first)
            def _():
                for i in range(own):
                    load(i, 2).wait()
        width = dim // 4
        base = (k * 2 + yy) * ne
        for n in range(4):
            cols = slice(n * width, (n + 1) * width)
            total = mm(inners[0], down[0, :, cols])
            for i in range(1, own):
                total = total + mm(inners[i], down[i, :, cols])
            for b in range(ne):
                part[base + b, :, cols] = total[b * rows : (b + 1) * rows].astype(bf16)
        near(k, yy, ao).start()
        near(k, yy, a).start()

    def second(k, yy, far):
        for aa, other in ((ao, True), (a, False)):
            f = (k * 2 + yy) * 2 + aa
            near(k, yy, aa).wait_recv()
            acc1[f] = (part[f * 2 + c].astype(f32) + near_in[f].astype(f32)).astype(bf16)
            if other:
                step_a(k, yy).start()
            if far:
                step_b(k, aa).start()

    def third(k):
        for far in (True, False):
            yy = yo if far else y
            aa = ao if far else a
            step_a(k, yy).wait_recv()
            i = k * 2 + yy
            acc2a[i] = (acc1[i * 2 + a, :, lo].astype(f32) + in_a[i].astype(f32)).astype(bf16)
            if far:
                step_a2(k).start()
            step_b(k, aa).wait_recv()
            i = k * 2 + aa
            acc2b[i] = (acc1[(k * 2 + y) * 2 + aa, :, hi].astype(f32) + in_b[i].astype(f32)).astype(bf16)
            if far:
                step_b2(k).start()

    def fourth(j):
        k = at(j)
        step_a2(k).wait_recv()
        acc3[j, :, lo] = (acc2a[k * 2 + y].astype(f32) + in2_a[k].astype(f32)).astype(bf16)
        step_b2(k).wait_recv()
        acc3[j, :, hi] = (acc2b[k * 2 + a].astype(f32) + in2_b[k].astype(f32)).astype(bf16)
        last(j).start()

    def lap(j, carry):
        k = at(j)
        fetch(k, y, 1).start()
        fetch(k, yo, 0).wait()
        tile(k, yo, 0, j == 0)

        @pl.when(j > 0)
        def _():
            second(at(j - 1), y, False)

        @pl.when(j > 1)
        def _():
            fourth(j - 2)

        @pl.when(j < nz - 1)
        def _():
            fetch(at(j + 1), yo, 0).start()

        fetch(k, y, 1).wait()
        tile(k, y, 1, None)
        second(k, yo, True)

        @pl.when(j > 0)
        def _():
            third(at(j - 1))

        return carry

    lax.fori_loop(0, nz, lap, 0)
    second(z, y, False)
    if nz > 1:
        fourth(nz - 2)
    third(z)
    step_a2(z).wait_recv()
    step_b2(z).wait_recv()
    left = acc2a[z * 2 + y].astype(f32) + in2_a[z].astype(f32)
    right = acc2b[z * 2 + a].astype(f32) + in2_b[z].astype(f32)
    for j in range(nz - 1):
        last(j).wait_recv()
        left = left + in3[j, :, lo].astype(f32)
        right = right + in3[j, :, hi].astype(f32)
    out_ref[:, lo] = left.astype(bf16)
    out_ref[:, hi] = right.astype(bf16)

    def drain(k, carry):
        for i in range(2):
            for aa in range(2):
                near(k, i, aa).wait_send()
            step_a(k, i).wait_send()
            step_b(k, i).wait_send()
        step_a2(k).wait_send()
        step_b2(k).wait_send()
        return carry

    lax.fori_loop(0, nz, drain, 0)
    for j in range(nz - 1):
        last(j).wait_send()


def expert_call(ns, ne, tokens, select, gate, up, down):
    rows, width = tokens.shape[1:]
    own, dim, ff = gate.shape
    nz = ns // 2
    half = dim // 2
    n = nz * 4
    dma = pltpu.SemaphoreType.DMA
    buf = lambda m, w: pltpu.VMEM((m, rows, w), bf16)
    counts = (n, 2 * nz, 2 * nz, nz, nz, nz - 1)
    return pl.pallas_call(
        functools.partial(expert_kernel, ns, ne),
        in_specs=[ANY, ANY, ANY, ANY, VMEM],
        out_specs=VMEM,
        out_shape=jax.ShapeDtypeStruct((rows, dim), bf16),
        scratch_shapes=[
            pltpu.VMEM(gate.shape, bf16), pltpu.VMEM(up.shape, bf16), pltpu.VMEM(down.shape, bf16),
            pltpu.VMEM((2, ne, rows, width), bf16),
            buf(2 * n, dim), buf(n, dim), buf(n, dim),
            buf(2 * nz, half), buf(2 * nz, half), buf(2 * nz, half), buf(2 * nz, half),
            buf(nz, half), buf(nz, half), buf(nz - 1, dim), buf(nz - 1, dim),
            dma((3, own)), dma((2,)),
        ] + [dma((m,)) for m in counts for _ in range(2)],
        compiler_params=pltpu.CompilerParams(
            collective_id=1, has_side_effects=True, vmem_limit_bytes=60 << 20
        ),
        name="experts_and_sum",
    )(tokens, gate, up, down, select)


def expert_mlp(arrived, expert_gate, expert_up, expert_down):
    gate_act = jnp.einsum(
        "secd,edf->secf", arrived, expert_gate, preferred_element_type=jnp.float32
    )
    up_act = jnp.einsum("secd,edf->secf", arrived, expert_up, preferred_element_type=jnp.float32)
    inner = (jax.nn.silu(gate_act) * up_act).astype(jnp.bfloat16)
    return jnp.einsum(
        "secf,efd->secd", inner, expert_down, preferred_element_type=jnp.float32
    ).astype(jnp.bfloat16)


def routed(moe_in, route_experts, route_weights, expert_gate, expert_up, expert_down):
    rows_dev, model_dim = moe_in.shape
    devices = lax.axis_size("seq") * lax.axis_size("exp")
    exp_dev = expert_gate.shape[0]
    expert_count = exp_dev * devices
    top_picks = route_experts.shape[1]
    capacity = 2 * ((rows_dev * top_picks + expert_count - 1) // expert_count)
    pick_count = rows_dev * top_picks
    linear_labels = route_experts.reshape(-1)
    expert_ids = jnp.arange(expert_count, dtype=jnp.int32)
    pick_table = (linear_labels[:, None] == expert_ids[None, :]).astype(jnp.bfloat16)
    row_index = lax.broadcasted_iota(jnp.int32, (pick_count, pick_count), 0)
    col_index = lax.broadcasted_iota(jnp.int32, (pick_count, pick_count), 1)
    earlier_picks = (row_index > col_index).astype(jnp.bfloat16)
    ranks = jnp.dot(earlier_picks, pick_table, preferred_element_type=jnp.float32)
    slot_index = jnp.take_along_axis(ranks, linear_labels[:, None], axis=1)[:, 0].astype(jnp.int32)
    position = linear_labels * capacity + slot_index
    source_row = (
        jnp.full((expert_count * capacity,), rows_dev, jnp.int32)
        .at[position]
        .set(jnp.arange(pick_count, dtype=jnp.int32) // top_picks)
    )
    padded_rows = jnp.concatenate([moe_in, jnp.zeros((1, model_dim), jnp.bfloat16)], axis=0)
    outgoing = padded_rows[source_row].reshape(devices, exp_dev, capacity, model_dim)
    finished = expert_mlp(
        lax.all_to_all(outgoing, ("seq", "exp"), split_axis=0, concat_axis=0, tiled=True),
        expert_gate,
        expert_up,
        expert_down,
    )
    returned = lax.all_to_all(finished, ("seq", "exp"), split_axis=0, concat_axis=0, tiled=True)
    flat_back = returned.reshape(expert_count * capacity, model_dim)
    picked = flat_back[position].reshape(rows_dev, top_picks, model_dim)
    shares = route_weights / jnp.sum(route_weights, axis=1, keepdims=True)
    expert_mixture = jnp.sum(picked.astype(jnp.float32) * shares[:, :, None], axis=1).astype(
        jnp.bfloat16
    )
    return expert_mixture


def body(
    query_proj,
    key_proj,
    value_proj,
    result_valve_maps,
    beta_logit,
    decay_logit,
    decay_rate,
    conv_query,
    conv_key,
    conv_value,
    norm_gain,
    output_weight,
    residual,
    post_gain,
    route_experts,
    route_weights,
    expert_gate,
    expert_up,
    expert_down,
):
    ns, ne = lax.axis_size("seq"), lax.axis_size("exp")
    tok_rows = query_proj.shape[0]
    head_dim = norm_gain.shape[0]
    rim_width = conv_query.shape[0] - 1
    edge = jnp.concatenate(
        [
            query_proj[tok_rows - rim_width :],
            key_proj[tok_rows - rim_width :],
            value_proj[tok_rows - rim_width :],
        ],
        axis=1,
    )
    leading = shifted(edge, "seq", 1).astype(jnp.float32)
    beta = jax.nn.sigmoid(beta_logit)
    log_decay = -decay_rate[None, :] * jax.nn.softplus(decay_logit)
    lo, lift, maps, writes = local_terms(
        query_proj, key_proj, value_proj, leading, conv_query, conv_key, conv_value, beta, log_decay, head_dim
    )
    rows, dim = residual.shape
    own = expert_gate.shape[0]
    experts = own * ns * ne
    lanes = -(-experts // 128) * 128
    dense = ne == 4 and ns % 2 == 0 and ns * ne * rows * dim * 2 <= 8 << 20 and own * ff_bytes(expert_gate) <= 12 << 20
    shares = route_weights / jnp.sum(route_weights, axis=1, keepdims=True)
    lane = jnp.arange(lanes, dtype=jnp.int32)
    table = jnp.sum(
        jnp.where(route_experts[:, :, None] == lane[None, None, :], shares[:, :, None], 0.0), axis=1
    ).astype(bf16)
    mixer_out, tokens = mixer_call(
        ns, ne, dense, lo, lift, maps, writes, result_valve_maps, norm_gain[None, :], output_weight, residual,
        post_gain[None, :], table,
    )
    if not dense:
        return mixer_out, routed(tokens, route_experts, route_weights, expert_gate, expert_up, expert_down)
    place = lax.axis_index("seq") * ne + lax.axis_index("exp")
    mine = place * own + jnp.arange(own, dtype=jnp.int32)
    select = (lane[None, :] == mine[:, None]).astype(f32)
    return mixer_out, expert_call(ns, ne, tokens, select, expert_gate, expert_up, expert_down)


def ff_bytes(weight):
    return 3 * weight.shape[1] * weight.shape[2] * 2


def solution(mesh):
    in_specs = (
        P("seq", "exp"),
        P("seq", "exp"),
        P("seq", "exp"),
        P("seq", "exp"),
        P("seq", "exp"),
        P("seq", "exp"),
        P("exp"),
        P(None, "exp"),
        P(None, "exp"),
        P(None, "exp"),
        P(),
        P("exp", None),
        P(("seq", "exp"), None),
        P(),
        P(("seq", "exp"), None),
        P(("seq", "exp"), None),
        P(("seq", "exp"), None, None),
        P(("seq", "exp"), None, None),
        P(("seq", "exp"), None, None),
    )
    out_specs = (P(("seq", "exp"), None), P(("seq", "exp"), None))
    return jax.shard_map(body, mesh=mesh, in_specs=in_specs, out_specs=out_specs, check_vma=False)
```

time: 733 us -> 193 us (0.26)
  waiting for transfers between devices: 237 us -> 0.01 us
  Pallas kernels: 0 us -> 172 us
  other arithmetic: 178 us -> 8.23 us
  blocking collectives: 121 us -> 0 us
  local copies, waits for them, and re-layouts: 93.6 us -> 7.03 us
  matrix products: 73.2 us -> 0 us
  between operations: 14.6 us -> 0.7 us
    pallas_call x0 -> x3, Pallas kernels: none -> 172 us  [the longest x1 87.1 us: mixer_call(): pl.pallas_call(functools.partial(mixer_kernel, ns, ne, gather), in_specs=...]
    another operation x5 -> x4, other arithmetic: 159 us -> 2 us  [the longest x4 158 us: block_terms(): jax.scipy.linalg.solve_triangular(identity + coupling, stacked, lower=Tru...]
    all_to_all x1 -> x0, blocking collectives: 121 us -> none  [body(): lax.all_to_all(outgoing, ('seq', 'exp'), split_axis=0, concat_axis=0, til...]
    all_to_all x1 -> x0, waiting for transfers between devices: 117 us -> none  [body(): lax.all_to_all(finished, ('seq', 'exp'), split_axis=0, concat_axis=0, til...]
    all_gather x2 -> x0, waiting for transfers between devices: 89 us -> none  [carried_in(): lax.all_gather(a.astype(kind), axis)]
    dot_general x27 -> x0, matrix products: 71.2 us -> none  [the longest x8 16.9 us: step_memory(): jnp.einsum('hvd,hde->hve', memory, block_map, precision=highest)]
    reduce_scatter x1 -> x0, waiting for transfers between devices: 31.4 us -> none  [body(): lax.psum_scatter(jnp.dot(normed, output_weight, preferred_element_type=jn...]
    reshape x9 -> x4, local copies, waits for them, and re-layouts: 28.1 us -> 2.33 us  [the longest x2 0.87 us: local_terms(): betag = beta.reshape(rows, groups, gh).transpose(1, 0, 2)]
  transfers between devices with their start and end apart: 5 -> 1, of which waited for: 4 -> 0; matrix products, arithmetic and copies ran while one was open for 4% -> 5% of each run, Pallas kernels for 0% -> 0%
where the time goes in v1:
time: 193 us
  Pallas kernels  172 us (89%)
  other arithmetic  8.23 us (4%)
  local copies, waits for them, and re-layouts  7.03 us (4%)
  starting transfers between devices  4.87 us (3%)
    pallas_call x1, Pallas kernels, mixer_call(): pl.pallas_call(functools.partial(mixer_kernel, ns, ne, gather), in_specs=...  87.1 us
    pallas_call x1, Pallas kernels, expert_call(): pl.pallas_call(functools.partial(expert_kernel, ns, ne), in_specs=[ANY, A...  64.8 us
    pallas_call x1, Pallas kernels, local_terms(): pl.pallas_call(functools.partial(local_kernel, hd), grid=(groups,), in_sp...  20 us
    ppermute x1, starting transfers between devices, shifted(): lax.ppermute(value, axis, [(source, source + steps) for source in range(l...  4.87 us
  transfers between devices with their start and end apart: 1, of which 0 were waited for; matrix products, arithmetic and copies ran while one was open for 5% of the time, Pallas kernels for 0%

profile of v1, /device:TPU:0, one launch (start us, length us, event | category | flops | bytes accessed | tf_op | source)
XLA Modules:
  0.0 192.7 jit_solution(6749325993998109157)
XLA Ops:
  0.6 0.7 slice.26
  1.4 0.7 slice.24
  2.1 0.7 slice.25
  2.8 4.9 %collective-permute-start = (bf16[3,2048]{1,0:T(4,128)(2,1)S(1)}, bf16[3,2048]{1,0:T(4,128)(2,1)S(1)}, u32[]{:S(2)}, u32[]{:S(2)}) collective-permute-start(bf16[3,2048]{1,0:T(4,128)(2,1)S(1)} %pad_maximum_fusion), channel_id=1, source_target_pairs={{0,4},{4,8},{8,12},{12,16},{16,20},{20,24},{24,28},{1,5},{5,9},{9,... | collective-permute-start | bytes 36872 | tf_op jit(solution)/shard_map/ppermute | solution.py:24
  7.7 0.7 neg.12
  8.3 0.8 floor_bitcast_fusion
  9.1 1.1 reduce-window.6
  10.2 0.2 slice_reduce_fusion
  10.4 0.1 add_bitcast_fusion
  10.5 0.7 add_divide_fusion
  11.2 0.7 reduce_sum.18
  11.9 0.7 broadcast_divide_fusion
  12.6 0.7 compare_convert_fusion.sel_ref
  13.3 1.5 select_reduce_fusion.share_ref
  14.9 0.8 copy.41.cum_ref
  15.7 0.6 reshape.41.cumt_ref
  16.3 0.9 copy.37
  17.2 0.0 collective-permute-done
  17.2 0.6 pad_convert_fusion.1
  17.8 0.6 pad_convert_fusion.hv_ref
  18.4 20.0 %block_terms.1 = (f32[256,1024]{1,0:T(8,128)}, f32[256,1024]{1,0:T(8,128)}, f32[8,128,128]{2,1,0:T(8,128)}, f32[8,128,128]{2,1,0:T(8,128)}) custom-call(bf16[256,512]{1,0:T(8,128)(2,1)} %q_ref.1, bf16[256,512]{1,0:T(8,128)(2,1)} %k_ref.1, bf16[256,1024]{1,0:T(8,128)(2,1)} %v_ref.1, f32[8,512]{1,0:T(8,128)} %get-tuple-element.15.hq_ref, ...), custom_call_target="tpu_custom_call" | custom-call | tf_op jit(solution)/shard_map/block_terms/pallas_call | solution.py:150
  38.4 87.1 %mixer_tail.1 = (bf16[64,2048]{1,0:T(8,128)(2,1)}, bf16[32,64,2176]{2,1,0:T(8,128)(2,1)}) custom-call(f32[256,1024]{1,0:T(8,128)} %get-tuple-element.8.lo_ref, f32[256,1024]{1,0:T(8,128)} %get-tuple-element.9.lift_ref, f32[8,128,128]{2,1,0:T(8,128)} %get-tuple-element.10.map_ref, f32[8,128,128]{2,1,0:T(8,128)} %get-tuple-element.11.write_ref, ...), custom_call_target="tpu_custom_call" | custom-call | tf_op jit(solution)/shard_map/mixer_tail/pallas_call | solution.py:361
  125.6 0.0 copy-start
  125.6 64.8 %experts_and_sum.1 = bf16[64,2048]{1,0:T(8,128)(2,1)} custom-call(bf16[32,64,2176]{2,1,0:T(8,128)(2,1)} %get-tuple-element.13.tok_ref, bf16[2,2048,512]{2,1,0:T(8,128)(2,1)} %gate_hbm.1, bf16[2,2048,512]{2,1,0:T(8,128)(2,1)} %up_hbm.1, bf16[2,512,2048]{2,1,0:T(8,128)(2,1)} %down_hbm.1, f32[2,128]{1,0:T(2,128)} %compare_convert_fusion.sel_ref), custom_call_target="tpu_custom_call" | custom-call | tf_op jit(solution)/shard_map/experts_and_sum/pallas_call | solution.py:581
  190.4 0.0 copy-done
  190.4 0.7 copy.44
  191.1 1.7 copy.45
  (9 shorter events, 0.1 us)
Async XLA Ops:
  2.8 14.4 %collective-permute-start = (bf16[3,2048]{1,0:T(4,128)(2,1)S(1)}, bf16[3,2048]{1,0:T(4,128)(2,1)S(1)}, u32[]{:S(2)}, u32[]{:S(2)}) collective-permute-start(bf16[3,2048]{1,0:T(4,128)(2,1)S(1)} %pad_maximum_fusion), channel_id=1, source_target_pairs={{0,4},{4,8},{8,12},{12,16},{16,20},{20,24},{24,28},{1,5},{5,9},{9,... | collective-permute-start | bytes 36872 | tf_op jit(solution)/shard_map/ppermute | solution.py:24
  125.6 64.8 %copy-start = (bf16[64,2048]{1,0:T(8,128)(2,1)S(1)}, bf16[64,2048]{1,0:T(8,128)(2,1)}, u32[]{:S(2)}) copy-start(bf16[64,2048]{1,0:T(8,128)(2,1)} %get-tuple-element.20) | copy-start | bytes 786436

commit v2 on v1

--- a/solution.py
+++ b/solution.py
@@ -47,7 +47,7 @@
     taps = w_ref.shape[0]
     rows = x_ref.shape[0]
     top = halo_ref.shape[0]
-    padded = jnp.concatenate([halo_ref[...], x_ref[...].astype(f32)], axis=0)
+    padded = jnp.concatenate([halo_ref[...].astype(f32), x_ref[...].astype(f32)], axis=0)
     total = w_ref[taps - 1 : taps, :] * padded[top : top + rows]
     for j in range(taps - 1):
         start = top - (taps - 1) + j
@@ -57,7 +57,7 @@
 
 def local_kernel(
     hd, q_ref, k_ref, v_ref, hq_ref, hk_ref, hv_ref, wq_ref, wk_ref, wv_ref,
-    beta_ref, cum_ref, cumt_ref, lo_ref, lift_ref, map_ref, write_ref, coup, inv, score,
+    logit_ref, decay_ref, rate_ref, lo_ref, lift_ref, map_ref, write_ref, coup, inv, score,
 ):
     rows = q_ref.shape[0]
     key_heads = q_ref.shape[1] // hd
@@ -71,6 +71,29 @@
     apart = ri ^ ci
     low = ri >= ci
     strict = ri > ci
+    group = pl.program_id(0)
+
+    def chosen(ref):
+        picked = ref[:, :heads]
+        for g in range(1, ref.shape[1] // heads):
+            picked = jnp.where(group == g, ref[:, g * heads : (g + 1) * heads], picked)
+        return picked
+
+    logit, decay_in, rate = chosen(logit_ref), chosen(decay_ref), chosen(rate_ref)
+    beta_all = 1.0 / (1.0 + jnp.exp(-logit))
+    log_decay = -rate * (jnp.maximum(decay_in, 0.0) + jnp.log1p(jnp.exp(-jnp.abs(decay_in))))
+    bounded = jnp.maximum(log_decay, -110.0)
+    whole = jnp.floor(bounded)
+    fraction = bounded - whole
+    f_high, f_rest = fraction.astype(bf16), fraction - fraction.astype(bf16).astype(f32)
+    f_mid, f_low = split(f_rest)
+    lower = jnp.where(low, 1.0, 0.0).astype(bf16)
+    upper = jnp.where(ri <= ci, 1.0, 0.0).astype(bf16)
+    whole = whole.astype(bf16)
+    cum_w = mm(lower, whole)
+    cum_f = mm(lower, f_high) + (mm(lower, f_mid) + mm(lower, f_low))
+    cumt_w = mm(whole, upper, TN)
+    cumt_f = mm(f_high, upper, TN) + (mm(f_mid, upper, TN) + mm(f_low, upper, TN))
     qs, ks = [], []
     for a in range(key_heads):
         ka = k[:, a * hd : (a + 1) * hd]
@@ -81,11 +104,9 @@
         kk = dot3(ka, ka, NT)
         qk = dot3(qa, ka, NT)
         for h in range(a * per, (a + 1) * per):
-            spread = (cum_ref[:, h : h + 1] - cumt_ref[h : h + 1, :]) + (
-                cum_ref[:, heads + h : heads + h + 1] - cumt_ref[heads + h : heads + h + 1, :]
-            )
+            spread = (cum_w[:, h : h + 1] - cumt_w[h : h + 1, :]) + (cum_f[:, h : h + 1] - cumt_f[h : h + 1, :])
             decay = jnp.where(low, jnp.exp(jnp.where(low, spread, 0.0)), 0.0)
-            coupling = jnp.where(strict, beta_ref[:, h : h + 1] * kk * decay, 0.0)
+            coupling = jnp.where(strict, beta_all[:, h : h + 1] * kk * decay, 0.0)
             coup[h] = coupling
             score[h] = qk * decay
             inv[h] = jnp.where(ri == ci, 1.0, 0.0) - jnp.where(apart == 1, coupling, 0.0)
@@ -109,14 +130,11 @@
         lax.broadcasted_iota(jnp.int32, (hd, hd), 0) == lax.broadcasted_iota(jnp.int32, (hd, hd), 1), 1.0, 0.0
     )
     for h in range(heads):
-        cum = cum_ref[:, h : h + 1] + cum_ref[:, heads + h : heads + h + 1]
-        growth = jnp.exp(cum)
-        last_w = cum_ref[rows - 1 : rows, h : h + 1]
-        last_f = cum_ref[rows - 1 : rows, heads + h : heads + h + 1]
-        remain = jnp.exp(
-            (last_w - cum_ref[:, h : h + 1]) + (last_f - cum_ref[:, heads + h : heads + h + 1])
-        )
-        beta = beta_ref[:, h : h + 1]
+        growth = jnp.exp(cum_w[:, h : h + 1] + cum_f[:, h : h + 1])
+        last_w = cum_w[rows - 1 : rows, h : h + 1]
+        last_f = cum_f[rows - 1 : rows, h : h + 1]
+        remain = jnp.exp((last_w - cum_w[:, h : h + 1]) + (last_f - cum_f[:, h : h + 1]))
+        beta = beta_all[:, h : h + 1]
         qa, ka = qs[h // per], ks[h // per]
         stacked = jnp.concatenate([beta * v[:, h * hd : (h + 1) * hd], (beta * growth) * ka], axis=1)
         solved = dot3(inv[h], stacked)
@@ -128,32 +146,27 @@
         map_ref[h] = jnp.exp(last_w + last_f) * eye - ends[hd:]
 
 
-def local_terms(q, k, v, halo, wq, wk, wv, beta, log_decay, hd):
+def local_terms(q, k, v, halo, wq, wk, wv, logit, decay, rate, hd):
     rows, kc = q.shape
     vc = v.shape[1]
     heads = vc // hd
-    groups = 2 if (kc // hd) % 2 == 0 else 1
+    groups = 2 if (kc // hd) % 2 == 0 and 2 * kc % vc == 0 else 1
     gh = heads // groups
     kw, vw = kc // groups, vc // groups
-    bounded = jnp.maximum(log_decay, -110.0)
-    whole = jnp.floor(bounded)
-    sums = jnp.cumsum(jnp.stack([whole, bounded - whole]), axis=1)
-    cum = sums.reshape(2, rows, groups, gh).transpose(2, 1, 0, 3).reshape(groups, rows, 2 * gh)
-    cumt = sums.reshape(2, rows, groups, gh).transpose(2, 0, 3, 1).reshape(groups, 2 * gh, rows)
-    betag = beta.reshape(rows, groups, gh).transpose(1, 0, 2)
-    taps = wq.shape[0]
-    halo = jnp.concatenate([jnp.zeros((8 - halo.shape[0], halo.shape[1]), f32), halo], axis=0)
-    hq, hk, hv = halo[:, :kc], halo[:, kc : 2 * kc], halo[:, 2 * kc :]
+    taps, top = wq.shape[0], halo.shape[0]
+    whole = lambda r: pl.BlockSpec((r, heads), lambda g: (0, 0))
     col = lambda r, w: pl.BlockSpec((r, w), lambda g: (0, g))
-    lead = lambda a, b: pl.BlockSpec((None, a, b), lambda g: (g, 0, 0))
     mats = pl.BlockSpec((gh, hd, hd), lambda g: (g, 0, 0))
     return pl.pallas_call(
         functools.partial(local_kernel, hd),
         grid=(groups,),
         in_specs=[
-            col(rows, kw), col(rows, kw), col(rows, vw), col(8, kw), col(8, kw), col(8, vw),
+            col(rows, kw), col(rows, kw), col(rows, vw),
+            pl.BlockSpec((top, kw), lambda g: (0, g)),
+            pl.BlockSpec((top, kw), lambda g: (0, kc // kw + g)),
+            pl.BlockSpec((top, vw), lambda g: (0, 2 * kc // vw + g)),
             col(taps, kw), col(taps, kw), col(taps, vw),
-            lead(rows, gh), lead(rows, 2 * gh), lead(2 * gh, rows),
+            whole(rows), whole(rows), whole(1),
         ],
         out_specs=[col(rows, vw), col(rows, vw), mats, mats],
         out_shape=[
@@ -165,13 +178,13 @@
         scratch_shapes=[pltpu.VMEM((gh, rows, rows), f32)] * 3,
         compiler_params=pltpu.CompilerParams(vmem_limit_bytes=60 << 20),
         name="block_terms",
-    )(q, k, v, hq, hk, hv, wq, wk, wv, betag, cum, cumt)
+    )(q, k, v, halo, halo, halo, wq, wk, wv, logit, decay, rate)
 
 
 def mixer_kernel(
-    ns, ne, gather, lo_ref, lift_ref, map_ref, write_ref, valve_ref, gain_ref, w_ref, res_ref, post_ref, share_ref,
-    out_ref, tok_ref, state_in, state_out, normed, partial, wire, near_in, cross_out, cross_in, payload,
-    st_send, st_recv, rs_send, rs_recv, xs_send, xs_recv, ag_send, ag_recv, own_sem,
+    ns, ne, gather, lo_ref, lift_ref, map_ref, write_ref, valve_ref, gain_ref, w_ref, res_ref, post_ref, pick_ref, weight_ref,
+    out_ref, tok_ref, state_in, state_out, normed, partial, wire, near_in, cross_out, cross_in,
+    st_send, st_recv, rs_send, rs_recv, xs_send, xs_recv,
 ):
     s = lax.axis_index("seq")
     e = lax.axis_index("exp")
@@ -196,6 +209,14 @@
     @pl.when(s == 0)
     def _():
         state_in[...] = jnp.zeros_like(state_in)
+
+    if gather:
+        shares = weight_ref[...] / jnp.sum(weight_ref[...], axis=1, keepdims=True)
+        lane = lax.broadcasted_iota(jnp.int32, (rows, tok_ref.shape[1] - dim), 1)
+        table = jnp.zeros(lane.shape, f32)
+        for pick in range(pick_ref.shape[1]):
+            table = table + jnp.where(pick_ref[:, pick : pick + 1] == lane, shares[:, pick : pick + 1], 0.0)
+        tok_ref[:, dim:] = table.astype(bf16)
 
     for h in range(heads):
         mh, ml = split(map_ref[h])
@@ -260,85 +281,7 @@
     tokens = (
         mixed * lax.rsqrt(jnp.mean(mixed * mixed, axis=1, keepdims=True) + epsilon) * post_ref[...]
     ).astype(bf16)
-    sends = []
-    if gather:
-        payload[:, :dim] = tokens
-        payload[:, dim:] = share_ref[...]
-        nz = ns // 2
-        z, y = s // 2, s % 2
-        here = (z, y, a, c)
-        half = dim // 2
-        spans = (pl.ds(0, half), pl.ds(half, payload.shape[1] - half))
-
-        def slot(p):
-            return ((p[0] * 2 + p[1]) * na + p[2]) * 2 + p[3]
-
-        own = pltpu.make_async_copy(payload, tok_ref.at[slot(here)], own_sem)
-        own.start()
-
-        def send(part, place, target, mine):
-            index = slot(place)
-            number = sum(1 for other, _ in sends if other == part)
-            source = payload if mine else tok_ref.at[index]
-            copy = pltpu.make_async_remote_copy(
-                src_ref=source.at[:, spans[part]], dst_ref=tok_ref.at[index, :, spans[part]],
-                send_sem=ag_send.at[part, number], recv_sem=ag_recv.at[part, index],
-                device_id=(target[0] * 2 + target[1], target[2] * 2 + target[3]), device_id_type=MESH,
-            )
-            copy.start()
-            sends.append((part, copy))
-
-        def arrive(part, place):
-            index = slot(place)
-            pltpu.make_async_remote_copy(
-                src_ref=payload.at[:, spans[part]], dst_ref=tok_ref.at[index, :, spans[part]],
-                send_sem=ag_send.at[part, 0], recv_sem=ag_recv.at[part, index],
-                device_id=(s, a * 2 + 1 - c), device_id_type=MESH,
-            ).wait_recv()
-
-        ypeer = (z, 1 - y, a, c)
-        xpeer = (z, y, 1 - a, c)
-        cpeer = (z, y, a, 1 - c)
-        first, second = (ypeer, xpeer), (xpeer, ypeer)
-        zs = [(z + i) % nz for i in range(nz)]
-        back = [(z - i + nz) % nz for i in range(nz)]
-        for i in range(1, nz):
-            for part in (0, 1):
-                send(part, here, (zs[i], y, a, c), True)
-        for peers in (first, second, (cpeer, cpeer)):
-            for part in (0, 1):
-                send(part, here, peers[part], True)
-        for i in range(1, nz):
-            for part in (0, 1):
-                place = (back[i], y, a, c)
-                arrive(part, place)
-                send(part, place, first[part], False)
-                send(part, place, second[part], False)
-                send(part, place, cpeer, False)
-        for i in range(nz):
-            for part in (0, 1):
-                place = (back[i],) + first[part][1:]
-                arrive(part, place)
-                send(part, place, second[part], False)
-                send(part, place, cpeer, False)
-        for via in (0, 1):
-            for i in range(nz):
-                for part in (0, 1):
-                    place = (back[i],) + second[part][1:]
-                    if via:
-                        place = (back[i], 1 - y, 1 - a, c)
-                    arrive(part, place)
-                    send(part, place, cpeer, False)
-        for yy in (y, 1 - y):
-            for aa in (a, 1 - a):
-                for i in range(nz):
-                    for part in (0, 1):
-                        arrive(part, (back[i], yy, aa, 1 - c))
-        own.wait()
-    else:
-        tok_ref[...] = tokens
-    for _, copy in sends:
-        copy.wait_send()
+    tok_ref[:, :dim] = tokens
     for h in range(heads):
         @pl.when(s < ns - 1)
         def _():
@@ -349,40 +292,37 @@
         cross(i).wait_send()
 
 
-def mixer_call(ns, ne, gather, lo, lift, maps, writes, valve, gain, weight, residual, post, shares):
+def mixer_call(ns, ne, gather, lo, lift, maps, writes, valve, gain, weight, residual, post, picks, pick_weights, lanes):
     heads, hd, _ = maps.shape
     tok_rows = lo.shape[0]
     rows, dim = residual.shape
     na = ne // 2
-    width = dim + shares.shape[1]
+    width = dim + lanes if gather else dim
     dma = pltpu.SemaphoreType.DMA
-    tok_shape = (ns * ne, rows, width) if gather else (rows, dim)
-    sent = (ns // 2 - 1) + 3 + 3 * (ns // 2 - 1) + 2 * (ns // 2) + 2 * (ns // 2)
     return pl.pallas_call(
         functools.partial(mixer_kernel, ns, ne, gather),
-        in_specs=[VMEM] * 10,
-        out_specs=[VMEM, ANY if gather else VMEM],
-        out_shape=[jax.ShapeDtypeStruct((rows, dim), bf16), jax.ShapeDtypeStruct(tok_shape, bf16)],
+        in_specs=[VMEM] * 11,
+        out_specs=[VMEM, VMEM],
+        out_shape=[jax.ShapeDtypeStruct((rows, dim), bf16), jax.ShapeDtypeStruct((rows, width), bf16)],
         scratch_shapes=[
             pltpu.VMEM((heads, hd, hd), bf16), pltpu.VMEM((heads, hd, hd), bf16),
             pltpu.VMEM((tok_rows, heads * hd), bf16),
             pltpu.VMEM((ne, rows, dim), f32), pltpu.VMEM((ne, rows, dim), bf16),
             pltpu.VMEM((na, rows, dim), bf16),
             pltpu.VMEM((na - 1, rows, dim), bf16), pltpu.VMEM((na - 1, rows, dim), bf16),
-            pltpu.VMEM((rows, width), bf16),
             dma((heads,)), dma((heads,)), dma((na,)), dma((na,)), dma((na - 1,)), dma((na - 1,)),
-            dma((2, sent)), dma((2, ns * ne)), dma,
         ],
         compiler_params=pltpu.CompilerParams(
             collective_id=0, has_side_effects=True, vmem_limit_bytes=60 << 20
         ),
         name="mixer_tail",
-    )(lo, lift, maps, writes, valve, gain, weight, residual, post, shares)
+    )(lo, lift, maps, writes, valve, gain, weight, residual, post, picks, pick_weights)
 
 
 def expert_kernel(
-    ns, ne, tok_ref, gate_hbm, up_hbm, down_hbm, sel_ref, out_ref, gate, up, down, xbuf, part, near_in, acc1,
+    ns, ne, payload, gate_hbm, up_hbm, down_hbm, out_ref, tok_ref, gate, up, down, xbuf, part, near_in, acc1,
     in_a, in_b, acc2a, acc2b, in2_a, in2_b, acc3, in3, w_sem, x_sem,
+    g_send, gz_send, g_recv, own_sem,
     n_send, n_recv, a_send, a_recv, b_send, b_recv, a2_send, a2_recv, b2_send, b2_recv, z_send, z_recv,
 ):
     s = lax.axis_index("seq")
@@ -407,9 +347,8 @@
         return pltpu.make_async_copy(tok_ref.at[pl.ds((k * 2 + yy) * ne, ne)], xbuf.at[place], x_sem.at[place])
 
     def at(j):
-        return (z + 1 + j) % nz
-
-    fetch(at(0), yo, 0).start()
+        return (z - j + nz) % nz
+
     for i in range(own):
         for kind in range(3):
             load(i, kind).start()
@@ -444,9 +383,74 @@
 
     def last(j):
         k = at(j)
-        return copy(acc3.at[j], in3.at[j], z_send.at[j], z_recv.at[j], (k * 2 + y, e))
-
-    def tile(k, yy, place, first):
+        return copy(acc3.at[j - 1], in3.at[j - 1], z_send.at[j - 1], z_recv.at[j - 1], (k * 2 + y, e))
+
+    cut = (pl.ds(0, half), pl.ds(half, payload.shape[1] - half))
+    routes = (((yo, a), (y, ao)), ((y, ao), (yo, a)))
+
+    def slot(k, yy, aa, cc):
+        return ((k * 2 + yy) * 2 + aa) * 2 + cc
+
+    def pass_on(half_at, j, number, place, target, mine=False):
+        source = payload.at[:, cut[half_at]] if mine else tok_ref.at[place, :, cut[half_at]]
+        return copy(
+            source, tok_ref.at[place, :, cut[half_at]], g_send.at[half_at, j, number], g_recv.at[half_at, place], target
+        )
+
+    def hop(half_at, step):
+        yy, aa = routes[half_at][step]
+        return (z * 2 + yy, aa * 2 + c)
+
+    def arrive(half_at, place):
+        pass_on(half_at, 0, 0, place, cpeer).wait_recv()
+
+    def stage(j, number, mine=False):
+        for half_at in (0, 1):
+            first_place, second_place = routes[half_at]
+            yy, aa = ((y, a), first_place, second_place, (yo, ao))[number]
+            place = slot(at(j), yy, aa, c)
+            if not mine:
+                arrive(half_at, place)
+            if number == 0:
+                pass_on(half_at, j, 0, place, hop(half_at, 0), mine).start()
+            if number < 2:
+                pass_on(half_at, j, 1 + number, place, hop(half_at, 1), mine).start()
+            pass_on(half_at, j, 3 + number, place, cpeer, mine).start()
+
+    def ended(j):
+        for number in range(7):
+            for half_at in (0, 1):
+                pass_on(half_at, j, number, 0, cpeer).wait_send()
+
+    def landed(j):
+        for yy in (y, yo):
+            for aa in (a, ao):
+                for half_at in (0, 1):
+                    arrive(half_at, slot(at(j), yy, aa, 1 - c))
+
+    def give(half_at, j):
+        place = slot(z, y, a, c)
+        return copy(
+            payload.at[:, cut[half_at]], tok_ref.at[place, :, cut[half_at]], gz_send.at[half_at, j - 1],
+            g_recv.at[half_at, place], (((z + j) % nz) * 2 + y, e),
+        )
+
+    mine_copy = pltpu.make_async_copy(payload, tok_ref.at[slot(z, y, a, c)], own_sem)
+    mine_copy.start()
+    stage(0, 0, True)
+    for j in range(1, nz):
+        for half_at in (0, 1):
+            give(half_at, j).start()
+    for number in (1, 2, 3):
+        stage(0, number)
+    if nz > 1:
+        stage(1, 0)
+    landed(0)
+    mine_copy.wait()
+
+    lane = lax.broadcasted_iota(jnp.int32, (ne * rows, xbuf.shape[-1] - dim), 1)
+
+    def tile(k, yy, place, first, between):
         x = xbuf[place].reshape(ne * rows, xbuf.shape[-1])
         spread = x[:, dim:].astype(f32)
         inners = []
@@ -456,10 +460,11 @@
                 def _():
                     load(i, 0).wait()
                     load(i, 1).wait()
-            share = jnp.sum(spread * sel_ref[i : i + 1, :], axis=1, keepdims=True)
+            share = jnp.sum(jnp.where(lane == (s * ne + e) * own + i, spread, 0.0), axis=1, keepdims=True)
             g = mm(x[:, :dim], gate[i])
             u = mm(x[:, :dim], up[i])
             inners.append((silu(g) * u * share).astype(bf16))
+        between()
         if first is not None:
             @pl.when(first)
             def _():
@@ -505,52 +510,68 @@
     def fourth(j):
         k = at(j)
         step_a2(k).wait_recv()
-        acc3[j, :, lo] = (acc2a[k * 2 + y].astype(f32) + in2_a[k].astype(f32)).astype(bf16)
+        acc3[j - 1, :, lo] = (acc2a[k * 2 + y].astype(f32) + in2_a[k].astype(f32)).astype(bf16)
         step_b2(k).wait_recv()
-        acc3[j, :, hi] = (acc2b[k * 2 + a].astype(f32) + in2_b[k].astype(f32)).astype(bf16)
+        acc3[j - 1, :, hi] = (acc2b[k * 2 + a].astype(f32) + in2_b[k].astype(f32)).astype(bf16)
         last(j).start()
 
     def lap(j, carry):
         k = at(j)
+        more = j < nz - 1
+        fetch(k, yo, 0).start()
         fetch(k, y, 1).start()
+
+        def after(number):
+            @pl.when(more)
+            def _():
+                stage(j + 1, number)
+
         fetch(k, yo, 0).wait()
-        tile(k, yo, 0, j == 0)
+        tile(k, yo, 0, j == 0, lambda: after(1))
 
         @pl.when(j > 0)
         def _():
             second(at(j - 1), y, False)
 
-        @pl.when(j > 1)
+        @pl.when(j > 2)
         def _():
             fourth(j - 2)
 
-        @pl.when(j < nz - 1)
+        after(2)
+        fetch(k, y, 1).wait()
+        tile(k, y, 1, None, lambda: after(3))
+
+        @pl.when(j < nz - 2)
         def _():
-            fetch(at(j + 1), yo, 0).start()
-
-        fetch(k, y, 1).wait()
-        tile(k, y, 1, None)
+            stage(j + 2, 0)
+
         second(k, yo, True)
 
         @pl.when(j > 0)
         def _():
             third(at(j - 1))
 
+        @pl.when(more)
+        def _():
+            landed(j + 1)
+
         return carry
 
     lax.fori_loop(0, nz, lap, 0)
-    second(z, y, False)
+    second(at(nz - 1), y, False)
+    if nz > 2:
+        fourth(nz - 2)
+    third(at(nz - 1))
     if nz > 1:
-        fourth(nz - 2)
-    third(z)
+        fourth(nz - 1)
     step_a2(z).wait_recv()
     step_b2(z).wait_recv()
     left = acc2a[z * 2 + y].astype(f32) + in2_a[z].astype(f32)
     right = acc2b[z * 2 + a].astype(f32) + in2_b[z].astype(f32)
-    for j in range(nz - 1):
+    for j in range(1, nz):
         last(j).wait_recv()
-        left = left + in3[j, :, lo].astype(f32)
-        right = right + in3[j, :, hi].astype(f32)
+        left = left + in3[j - 1, :, lo].astype(f32)
+        right = right + in3[j - 1, :, hi].astype(f32)
     out_ref[:, lo] = left.astype(bf16)
     out_ref[:, hi] = right.astype(bf16)
 
@@ -562,15 +583,18 @@
             step_b(k, i).wait_send()
         step_a2(k).wait_send()
         step_b2(k).wait_send()
+        ended(k)
         return carry
 
     lax.fori_loop(0, nz, drain, 0)
-    for j in range(nz - 1):
+    for j in range(1, nz):
         last(j).wait_send()
-
-
-def expert_call(ns, ne, tokens, select, gate, up, down):
-    rows, width = tokens.shape[1:]
+        for half_at in (0, 1):
+            give(half_at, j).wait_send()
+
+
+def expert_call(ns, ne, tokens, gate, up, down):
+    rows, width = tokens.shape
     own, dim, ff = gate.shape
     nz = ns // 2
     half = dim // 2
@@ -580,9 +604,12 @@
     counts = (n, 2 * nz, 2 * nz, nz, nz, nz - 1)
     return pl.pallas_call(
         functools.partial(expert_kernel, ns, ne),
-        in_specs=[ANY, ANY, ANY, ANY, VMEM],
-        out_specs=VMEM,
-        out_shape=jax.ShapeDtypeStruct((rows, dim), bf16),
+        in_specs=[VMEM, ANY, ANY, ANY],
+        out_specs=[VMEM, ANY],
+        out_shape=[
+            jax.ShapeDtypeStruct((rows, dim), bf16),
+            jax.ShapeDtypeStruct((ns * ne, rows, width), bf16),
+        ],
         scratch_shapes=[
             pltpu.VMEM(gate.shape, bf16), pltpu.VMEM(up.shape, bf16), pltpu.VMEM(down.shape, bf16),
             pltpu.VMEM((2, ne, rows, width), bf16),
@@ -590,12 +617,13 @@
             buf(2 * nz, half), buf(2 * nz, half), buf(2 * nz, half), buf(2 * nz, half),
             buf(nz, half), buf(nz, half), buf(nz - 1, dim), buf(nz - 1, dim),
             dma((3, own)), dma((2,)),
+            dma((2, nz, 7)), dma((2, nz - 1)), dma((2, ns * ne)), dma,
         ] + [dma((m,)) for m in counts for _ in range(2)],
         compiler_params=pltpu.CompilerParams(
             collective_id=1, has_side_effects=True, vmem_limit_bytes=60 << 20
         ),
         name="experts_and_sum",
-    )(tokens, gate, up, down, select)
+    )(tokens, gate, up, down)[0]
 
 
 def expert_mlp(arrived, expert_gate, expert_up, expert_down):
@@ -673,7 +701,7 @@
     ns, ne = lax.axis_size("seq"), lax.axis_size("exp")
     tok_rows = query_proj.shape[0]
     head_dim = norm_gain.shape[0]
-    rim_width = conv_query.shape[0] - 1
+    rim_width = -(-(conv_query.shape[0] - 1) // 8) * 8
     edge = jnp.concatenate(
         [
             query_proj[tok_rows - rim_width :],
@@ -682,32 +710,23 @@
         ],
         axis=1,
     )
-    leading = shifted(edge, "seq", 1).astype(jnp.float32)
-    beta = jax.nn.sigmoid(beta_logit)
-    log_decay = -decay_rate[None, :] * jax.nn.softplus(decay_logit)
+    leading = shifted(edge, "seq", 1)
     lo, lift, maps, writes = local_terms(
-        query_proj, key_proj, value_proj, leading, conv_query, conv_key, conv_value, beta, log_decay, head_dim
+        query_proj, key_proj, value_proj, leading, conv_query, conv_key, conv_value, beta_logit, decay_logit,
+        decay_rate[None, :], head_dim,
     )
     rows, dim = residual.shape
     own = expert_gate.shape[0]
     experts = own * ns * ne
     lanes = -(-experts // 128) * 128
     dense = ne == 4 and ns % 2 == 0 and ns * ne * rows * dim * 2 <= 8 << 20 and own * ff_bytes(expert_gate) <= 12 << 20
-    shares = route_weights / jnp.sum(route_weights, axis=1, keepdims=True)
-    lane = jnp.arange(lanes, dtype=jnp.int32)
-    table = jnp.sum(
-        jnp.where(route_experts[:, :, None] == lane[None, None, :], shares[:, :, None], 0.0), axis=1
-    ).astype(bf16)
     mixer_out, tokens = mixer_call(
         ns, ne, dense, lo, lift, maps, writes, result_valve_maps, norm_gain[None, :], output_weight, residual,
-        post_gain[None, :], table,
+        post_gain[None, :], route_experts, route_weights, lanes,
     )
     if not dense:
         return mixer_out, routed(tokens, route_experts, route_weights, expert_gate, expert_up, expert_down)
-    place = lax.axis_index("seq") * ne + lax.axis_index("exp")
-    mine = place * own + jnp.arange(own, dtype=jnp.int32)
-    select = (lane[None, :] == mine[:, None]).astype(f32)
-    return mixer_out, expert_call(ns, ne, tokens, select, expert_gate, expert_up, expert_down)
+    return mixer_out, expert_call(ns, ne, tokens, expert_gate, expert_up, expert_down)
 
 
 def ff_bytes(weight):

time: 193 us -> 188 us (0.974)
  other arithmetic: 8.23 us -> 0.01 us
  local copies, waits for them, and re-layouts: 7.03 us -> 10.8 us
  Pallas kernels: 172 us -> 170 us
    pallas_call x1, Pallas kernels: 87.1 us -> 20.6 us  [mixer_call(): pl.pallas_call(functools.partial(mixer_kernel, ns, ne, gather), in_specs=...]
    pallas_call x1, Pallas kernels: 64.8 us -> 129 us  [expert_call(): pl.pallas_call(functools.partial(expert_kernel, ns, ne), in_specs=[VMEM,...]
    unnamed x4 -> x10, local copies, waits for them, and re-layouts: 2.38 us -> 8.72 us
    reshape x4 -> x0, local copies, waits for them, and re-layouts: 2.33 us -> none  [the longest x2 0.87 us: local_terms(): betag = beta.reshape(rows, groups, gh).transpose(1, 0, 2)]
    reduce_sum x2 -> x0, other arithmetic: 2.26 us -> none  [the longest x1 1.54 us: body(): jnp.sum(jnp.where(route_experts[:, :, None] == lane[None, None, :], share...]
    another operation x4 -> x0, other arithmetic: 2 us -> none
  transfers between devices with their start and end apart: 1 -> 1, of which waited for: 0 -> 0; matrix products, arithmetic and copies ran while one was open for 5% -> 3% of each run, Pallas kernels for 0% -> 0%
where the time goes in v2:
time: 188 us; the launch traced here: 187 us
  Pallas kernels  170 us (90%)
  local copies, waits for them, and re-layouts  10.8 us (6%)
  starting transfers between devices  4.86 us (3%)
    pallas_call x1, Pallas kernels, expert_call(): pl.pallas_call(functools.partial(expert_kernel, ns, ne), in_specs=[VMEM,...  129 us
    pallas_call x1, Pallas kernels, local_terms(): pl.pallas_call(functools.partial(local_kernel, hd), grid=(groups,), in_sp...  20.7 us
    pallas_call x1, Pallas kernels, mixer_call(): pl.pallas_call(functools.partial(mixer_kernel, ns, ne, gather), in_specs=...  20.6 us
    unnamed x10, local copies, waits for them, and re-layouts  8.72 us
    ppermute x1, starting transfers between devices, shifted(): lax.ppermute(value, axis, [(source, source + steps) for source in range(l...  4.86 us
  transfers between devices with their start and end apart: 1, of which 0 were waited for; matrix products, arithmetic and copies ran while one was open for 3% of the time, Pallas kernels for 0%

profile of v2, /device:TPU:0, one launch (start us, length us, event | category | flops | bytes accessed | tf_op | source)
XLA Modules:
  0.0 186.7 jit_solution(11299228413220265936)
XLA Ops:
  0.6 0.7 slice.9
  1.3 0.7 slice.10
  2.0 0.7 slice.11
  2.8 4.9 %collective-permute-start = (bf16[8,2048]{1,0:T(8,128)(2,1)S(1)}, bf16[8,2048]{1,0:T(8,128)(2,1)S(1)}, u32[]{:S(2)}, u32[]{:S(2)}) collective-permute-start(bf16[8,2048]{1,0:T(8,128)(2,1)S(1)} %pad_maximum_fusion), channel_id=1, source_target_pairs={{0,4},{4,8},{8,12},{12,16},{16,20},{20,24},{24,28},{1,5},{5,9},{9,... | collective-permute-start | bytes 98312 | tf_op jit(solution)/shard_map/ppermute | solution.py:24
  7.6 1.4 copy.23.pick_ref
  9.0 1.4 copy.24.weight_ref
  10.4 1.5 copy.21.logit_ref
  11.9 1.5 copy.22.decay_ref
  13.4 0.0 collective-permute-done.hq_ref.hk_ref.hv_ref
  13.4 0.0 copy-start
  13.4 0.6 copy-done
  14.0 20.7 %block_terms.1 = (f32[256,1024]{1,0:T(8,128)}, f32[256,1024]{1,0:T(8,128)}, f32[8,128,128]{2,1,0:T(8,128)}, f32[8,128,128]{2,1,0:T(8,128)}) custom-call(bf16[256,512]{1,0:T(8,128)(2,1)} %q_ref.1, bf16[256,512]{1,0:T(8,128)(2,1)} %k_ref.1, bf16[256,1024]{1,0:T(8,128)(2,1)} %v_ref.1, bf16[8,2048]{1,0:T(8,128)(2,1)} %copy-done, bf16[8,2048]{1,0:T(8,128)(2,1)} %copy-done, ...), custom_call_target="tpu_custom_call" | custom-call | tf_op jit(solution)/shard_map/block_terms/pallas_call | solution.py:160
  34.7 20.6 %mixer_tail.1 = (bf16[64,2048]{1,0:T(8,128)(2,1)}, bf16[64,2176]{1,0:T(8,128)(2,1)}) custom-call(f32[256,1024]{1,0:T(8,128)} %get-tuple-element.9.lo_ref, f32[256,1024]{1,0:T(8,128)} %get-tuple-element.10.lift_ref, f32[8,128,128]{2,1,0:T(8,128)} %get-tuple-element.11.map_ref, f32[8,128,128]{2,1,0:T(8,128)} %get-tuple-element.12.write_ref, ...), custom_call_target="tpu_custom_call" | custom-call | tf_op jit(solution)/shard_map/mixer_tail/pallas_call | solution.py:302
  55.3 0.0 copy-start.1
  55.3 129.0 %experts_and_sum.1 = (bf16[64,2048]{1,0:T(8,128)(2,1)}, bf16[32,64,2176]{2,1,0:T(8,128)(2,1)}) custom-call(bf16[64,2176]{1,0:T(8,128)(2,1)} %get-tuple-element.14.payload, bf16[2,2048,512]{2,1,0:T(8,128)(2,1)} %gate_hbm.1, bf16[2,2048,512]{2,1,0:T(8,128)(2,1)} %up_hbm.1, bf16[2,512,2048]{2,1,0:T(8,128)(2,1)} %down_hbm.1), custom_call_target="tpu_custom_call" | custom-call | tf_op jit(solution)/shard_map/experts_and_sum/pallas_call | solution.py:605
  184.3 0.0 copy-done.1
  184.4 0.7 copy.27
  185.1 1.7 copy.28
  (1 shorter events, 0.0 us)
Async XLA Ops:
  2.8 10.6 %collective-permute-start = (bf16[8,2048]{1,0:T(8,128)(2,1)S(1)}, bf16[8,2048]{1,0:T(8,128)(2,1)S(1)}, u32[]{:S(2)}, u32[]{:S(2)}) collective-permute-start(bf16[8,2048]{1,0:T(8,128)(2,1)S(1)} %pad_maximum_fusion), channel_id=1, source_target_pairs={{0,4},{4,8},{8,12},{12,16},{16,20},{20,24},{24,28},{1,5},{5,9},{9,... | collective-permute-start | bytes 98312 | tf_op jit(solution)/shard_map/ppermute | solution.py:24
  13.4 0.6 copy-start
  55.3 129.0 %copy-start.1 = (bf16[64,2048]{1,0:T(8,128)(2,1)S(1)}, bf16[64,2048]{1,0:T(8,128)(2,1)}, u32[]{:S(2)}) copy-start(bf16[64,2048]{1,0:T(8,128)(2,1)} %get-tuple-element.18) | copy-start | bytes 786436
